TPU v7x, 128 devices: a whole 4x4x4 slice. The times are simulated.
128 devices in a mesh: chan: 32 (over z_lo, y, x), win: 4 (over z_hi, core).
Axes of the slice: x: 4, y: 4, z: 4 (z_hi: 2, z_lo: 2; z = z_hi * 2 + z_lo), core: 2. Of those that a mesh axis runs over, the one named last changes fastest.
Arguments:
- spectra: bfloat16 [2, 20, 512, 1536], P(None, 'win', 'chan'), may hold values from -40 to 40
- partners: int32 [512, 256], P('chan'), may hold values from 0 to 511, as said below
- pair_mask: int32 [512, 256], P('chan'), may hold values from 0 to 1, as said below
- gap_flags: int32 [512], P('chan'), may hold values 0 or 1
Outputs:
- lags: float32 [256, 512, 256], P('win', 'chan')
Inputs may be any that keep to these rules, and one draw needn't show every extreme that they name: `partners`: the 256 slots of channel c hold the channels c + o for every offset o from -128 to 128 but 0, in an order drawn from the seed; a slot whose offset leaves the cable holds c itself. `pair_mask`: 1 exactly where the slot's offset is at most 100 in magnitude and its channel lies on the cable.
All inputs are finite; a program needn't handle non-finite values. No bound on the sum of `gap_flags` on one device may be relied on, other than what follows from the above.
Results may differ from a plain program's by a relative error of at most 0.0041.
Values may be sent and summed in bfloat16 or wider, within the bound.
A program may use at most 128 MiB of HBM per device.

v0:
```python
import math

import jax
import jax.numpy as jnp
from jax import lax
from jax.sharding import PartitionSpec as P

LAGS = 256
SMOOTH = 8
FLO = 64
NSAMP = 6000


water_level = 0.1


def passed_along(value, axis, steps):
    count = lax.axis_size(axis)
    first, last = (max(0, -steps), min(count, count - steps))
    return lax.ppermute(value, axis, [(source, source + steps) for source in range(first, last)])


def whiten(spectra, gap_flags, half_width):
    real_part = spectra[0].astype(jnp.float32)
    imag_part = spectra[1].astype(jnp.float32)
    magnitude = jnp.sqrt(real_part * real_part + imag_part * imag_part)
    bins = magnitude.shape[-1]
    padded = jnp.pad(magnitude, ((0, 0), (0, 0), (half_width, half_width)))
    window_sum = padded[..., 0:bins]
    for offset_bin in range(1, 2 * half_width + 1):
        window_sum = window_sum + padded[..., offset_bin : offset_bin + bins]
    positions = jnp.arange(bins, dtype=jnp.int32)
    bin_count = (
        jnp.minimum(positions + half_width, bins - 1) - jnp.maximum(positions - half_width, 0) + 1
    ).astype(jnp.float32)
    smooth = window_sum / bin_count
    band_mean = jnp.mean(magnitude, axis=-1, keepdims=True)
    divisor = smooth + water_level * band_mean + 1e-06
    live_channel = (gap_flags == 0).astype(jnp.float32)[None, :, None]
    return jnp.stack(
        [real_part / divisor * live_channel, imag_part / divisor * live_channel]
    ).astype(jnp.bfloat16)


def lag_table(first_bin, bin_total, total_bins):
    bins = first_bin + jnp.arange(bin_total, dtype=jnp.int32)
    offsets = jnp.arange(LAGS, dtype=jnp.int32) - LAGS // 2
    phase_steps = jnp.mod((FLO + bins)[:, None] * offsets[None, :], NSAMP)
    angles = phase_steps.astype(jnp.float32) * (2.0 * math.pi / NSAMP)
    return jnp.concatenate([jnp.cos(angles), -jnp.sin(angles)], 0) / math.sqrt(total_bins)


def on_device(spectra, partners, pair_mask, gap_flags):
    channels = spectra.shape[2]
    slots = partners.shape[1]
    reach_span = slots // 2
    block_count = reach_span // channels
    whitened = whiten(spectra, gap_flags, SMOOTH)
    first_bin = 0
    windows = whitened.shape[1] * lax.axis_size("win")
    below_blocks = []
    above_blocks = []
    for distance in range(block_count):
        below_blocks.append(passed_along(whitened, "chan", distance + 1))
        above_blocks.append(passed_along(whitened, "chan", -(distance + 1)))
    extended = jnp.concatenate(below_blocks[::-1] + [whitened] + above_blocks, axis=2)
    local_bins = whitened.shape[3]
    basis = lag_table(first_bin, local_bins, spectra.shape[3])
    lag_count = basis.shape[1]
    group = min(32, slots)

    def one_offset(offset_slot):
        shift_by = jnp.where(
            offset_slot < reach_span, offset_slot - reach_span, offset_slot - reach_span + 1
        )
        partner_rows = lax.dynamic_slice_in_dim(extended, shift_by + reach_span, channels, 2)
        cross_real = jnp.einsum(
            "wcf,wcf->cf", whitened[0], partner_rows[0], preferred_element_type=jnp.float32
        ) + jnp.einsum(
            "wcf,wcf->cf", whitened[1], partner_rows[1], preferred_element_type=jnp.float32
        )
        cross_imag = jnp.einsum(
            "wcf,wcf->cf", whitened[1], partner_rows[0], preferred_element_type=jnp.float32
        ) - jnp.einsum(
            "wcf,wcf->cf", whitened[0], partner_rows[1], preferred_element_type=jnp.float32
        )
        return jnp.concatenate([cross_real, cross_imag], -1)

    def offset_block(block_number):
        offset_slots = block_number * group + jnp.arange(group, dtype=jnp.int32)
        joined = jax.vmap(one_offset)(offset_slots)
        joined = joined.reshape(group * channels, 2 * local_bins)
        result = jnp.dot(
            joined, basis, precision=lax.Precision.HIGHEST, preferred_element_type=jnp.float32
        )
        return result.reshape(group, channels, lag_count)

    by_offset = lax.map(offset_block, jnp.arange(slots // group, dtype=jnp.int32))
    by_offset = by_offset.reshape(slots, channels, lag_count)
    own_channel = lax.axis_index("chan") * channels + jnp.arange(channels, dtype=jnp.int32)
    relative = partners - own_channel[:, None]
    offset_index = jnp.where(relative < 0, relative + reach_span, relative + reach_span - 1)
    offset_index = jnp.clip(offset_index, 0, slots - 1)
    weights = pair_mask.astype(jnp.float32) / math.sqrt(windows)
    offset_ids = jnp.arange(slots, dtype=jnp.int32)
    picker = (offset_index[:, :, None] == offset_ids[None, None, :]).astype(jnp.float32) * weights[
        :, :, None
    ]
    return lax.psum_scatter(
        jnp.einsum(
            "cjo,oct->jct",
            picker,
            by_offset,
            precision=lax.Precision.HIGHEST,
            preferred_element_type=jnp.float32,
        ),
        "win",
        scatter_dimension=0,
        tiled=True,
    )


def solution(mesh):
    placed = (P(None, "win", "chan", None), P("chan", None), P("chan", None), P("chan"))
    return jax.shard_map(
        on_device, mesh=mesh, in_specs=placed, out_specs=P("win", "chan", None), check_vma=False
    )
```

profile of v0, /device:TPU:1, one launch (start us, length us, event | category | flops | bytes accessed | tf_op | source)
XLA Modules:
  0.0 807.7 jit_solution(10382958670183107140)
XLA Ops:
  6.5 1.3 fusion.39
  8.6 3.1 fusion.51
  12.8 5.7 collective-permute-start
  18.5 4.5 collective-permute-start.1
  23.0 4.5 collective-permute-start.2
  27.5 3.5 collective-permute-start.3
  31.0 2.9 collective-permute-start.4
  34.0 6.4 fusion.36
  40.4 1.9 maximum_multiply_fusion
  43.6 16.4 %collective-permute-done = bf16[2,5,16,1536]{3,2,1,0:T(8,128)(2,1)S(1)} collective-permute-done((bf16[2,5,16,1536]{3,2,1,0:T(8,128)(2,1)S(1)}, bf16[2,5,16,1536]{3,2,1,0:T(8,128)(2,1)S(1)}, u32[]{:S(2)}, u32[]{:S(2)}) %collective-permute-start) | collective-permute-done | bytes 491552 | tf_op jit(solution)/shard_map/ppermute | solution.py:20
  60.0 4.4 collective-permute-start.5
  64.4 1.6 collective-permute-start.6
  66.1 2.8 collective-permute-start.7
  69.0 1.3 collective-permute-start.8
  70.3 31.8 %collective-permute-done.4 = bf16[2,5,16,1536]{3,2,1,0:T(8,128)(2,1)S(1)} collective-permute-done((bf16[2,5,16,1536]{3,2,1,0:T(8,128)(2,1)S(1)}, bf16[2,5,16,1536]{3,2,1,0:T(8,128)(2,1)S(1)}, u32[]{:S(2)}, u32[]{:S(2)}) %collective-permute-start.4) | collective-permute-done | bytes 491552 | tf_op jit(solution)/shard_map/ppermute | solution.py:20
  102.1 1.3 collective-permute-start.9
  103.5 1.3 collective-permute-start.10
  104.8 1.3 collective-permute-start.11
  106.2 1.3 collective-permute-start.12
  107.6 1.3 collective-permute-start.13
  108.9 7.8 collective-permute-done.9
  116.7 1.6 collective-permute-start.14
  118.4 10.8 %collective-permute-done.10 = bf16[2,5,16,1536]{3,2,1,0:T(8,128)(2,1)S(1)} collective-permute-done((bf16[2,5,16,1536]{3,2,1,0:T(8,128)(2,1)S(1)}, bf16[2,5,16,1536]{3,2,1,0:T(8,128)(2,1)S(1)}, u32[]{:S(2)}, u32[]{:S(2)}) %collective-permute-start.10) | collective-permute-done | bytes 491552 | tf_op jit(solution)/shard_map/ppermute | solution.py:20
  129.2 1.3 collective-permute-start.15
  130.5 1.6 collective-permute-done.11
  132.2 7.5 collective-permute-done.13
  139.8 12.3 %collective-permute-done.14 = bf16[2,5,16,1536]{3,2,1,0:T(8,128)(2,1)S(1)} collective-permute-done((bf16[2,5,16,1536]{3,2,1,0:T(8,128)(2,1)S(1)}, bf16[2,5,16,1536]{3,2,1,0:T(8,128)(2,1)S(1)}, u32[]{:S(2)}, u32[]{:S(2)}) %collective-permute-start.14) | collective-permute-done | bytes 491552 | tf_op jit(solution)/shard_map/ppermute | solution.py:20
  152.2 30.1 %copy.8 = bf16[2,5,272,1536]{3,1,0,2:T(8,128)(2,1)} copy(bf16[2,5,272,1536]{3,2,1,0:T(8,128)(2,1)S(1)} %constant_dynamic-update-slice_fusion) | data formatting | bytes 16711680 | tf_op jit(solution)/shard_map/while | solution.py:98
  182.3 516.4 %while.14 = (s32[]{:T(128)}, f32[8,32,16,256]{3,2,1,0:T(8,128)}, s32[8]{0:T(128)S(1)}, bf16[2,5,272,1536]{3,1,0,2:T(8,128)(2,1)}, bf16[2,5,16,1536]{3,2,1,0:T(8,...) while((s32[]{:T(128)}, f32[8,32,16,256]{3,2,1,0:T(8,128)}, s32[8]{0:T(128)S(1)}, ...), condition=%wide.region_2.3_spmd, body=%wide.region_1.2_spmd.sunk | while | flops 4871406080 | bytes 93029936 | solution.py:98
  183.5 15.1 %gather_fusion = bf16[32,2,5,16,1536]{4,2,1,3,0:T(8,128)(2,1)} fusion(bf16[2,5,272,1536]{3,1,0,2:T(8,128)(2,1)} %get-tuple-element.241, s32[32]{0:T(128)S(1)} %shift-left_bitcast_fusion.2), kind=kCustom, calls=%fused_computation.clone.1 | custom fusion | bytes 31457792 | tf_op jit(solution)/shard_map/while/body/eval_jaxpr/vmap()/gather | solution.py:76
  199.4 35.7 %fusion.65 = (f32[16,1536,32]{1,0,2:T(8,128)S(1)}, f32[16,1536,32]{1,0,2:T(8,128)S(1)}, f32[16,1536,32]{1,0,2:T(8,128)S(1)}, f32[16,1536,32]{1,0,2:T(8,128)S(1)}) fusion(f32[16,1536,5]{1,2,0:T(8,128)S(1)} %copy.49, bf16[32,2,5,16,1536]{4,2,1,3,0:T(8,128)(2,1)} %gather_fusion, f32[16,1536,5]{1,2,0:T(8,128)S(1)} %copy.50), kind=kLoop, calls=%fused_computation.7.clone.1 | loop fusion | flops 36175872 | bytes 29294592 | tf_op jit(solution)/shard_map/while/body/eval_jaxpr/vmap(wcf,wcf->cf)/dot_general | solution.py:79
  235.1 3.0 subtract_bitcast_fusion.2
  238.1 8.7 %fusion.66 = f32[8,32,16,256]{3,2,1,0:T(8,128)} fusion(f32[8,32,16,256]{3,2,1,0:T(8,128)} %get-tuple-element.231, s32[]{:T(128)} %get-tuple-element.230, f32[3072,256]{1,0:T(8,128)} %get-tuple-element.243, f32[32,16,1536]{2,1,0:T(8,128)S(1)} %get-tuple-element.220, f32[32,16,1536]{2,1,0:T(8,128)} %get-tuple-element.221), kind=kOutput, calls=%fused_computation.19.clone.1 | convolution fusion | flops 4833411072 | bytes 9961984 | tf_op jit(solution)/shard_map/while/body/eval_jaxpr/dot_general | solution.py:93
  248.0 15.1 %gather_fusion = bf16[32,2,5,16,1536]{4,2,1,3,0:T(8,128)(2,1)} fusion(bf16[2,5,272,1536]{3,1,0,2:T(8,128)(2,1)} %get-tuple-element.241, s32[32]{0:T(128)S(1)} %shift-left_bitcast_fusion.2), kind=kCustom, calls=%fused_computation.clone.1 | custom fusion | bytes 31457792 | tf_op jit(solution)/shard_map/while/body/eval_jaxpr/vmap()/gather | solution.py:76
  263.9 35.7 %fusion.65 = (f32[16,1536,32]{1,0,2:T(8,128)S(1)}, f32[16,1536,32]{1,0,2:T(8,128)S(1)}, f32[16,1536,32]{1,0,2:T(8,128)S(1)}, f32[16,1536,32]{1,0,2:T(8,128)S(1)}) fusion(f32[16,1536,5]{1,2,0:T(8,128)S(1)} %copy.49, bf16[32,2,5,16,1536]{4,2,1,3,0:T(8,128)(2,1)} %gather_fusion, f32[16,1536,5]{1,2,0:T(8,128)S(1)} %copy.50), kind=kLoop, calls=%fused_computation.7.clone.1 | loop fusion | flops 36175872 | bytes 29294592 | tf_op jit(solution)/shard_map/while/body/eval_jaxpr/vmap(wcf,wcf->cf)/dot_general | solution.py:79
  299.6 3.0 subtract_bitcast_fusion.2
  302.7 8.7 %fusion.66 = f32[8,32,16,256]{3,2,1,0:T(8,128)} fusion(f32[8,32,16,256]{3,2,1,0:T(8,128)} %get-tuple-element.231, s32[]{:T(128)} %get-tuple-element.230, f32[3072,256]{1,0:T(8,128)} %get-tuple-element.243, f32[32,16,1536]{2,1,0:T(8,128)S(1)} %get-tuple-element.220, f32[32,16,1536]{2,1,0:T(8,128)} %get-tuple-element.221), kind=kOutput, calls=%fused_computation.19.clone.1 | convolution fusion | flops 4833411072 | bytes 9961984 | tf_op jit(solution)/shard_map/while/body/eval_jaxpr/dot_general | solution.py:93
  312.6 15.1 %gather_fusion = bf16[32,2,5,16,1536]{4,2,1,3,0:T(8,128)(2,1)} fusion(bf16[2,5,272,1536]{3,1,0,2:T(8,128)(2,1)} %get-tuple-element.241, s32[32]{0:T(128)S(1)} %shift-left_bitcast_fusion.2), kind=kCustom, calls=%fused_computation.clone.1 | custom fusion | bytes 31457792 | tf_op jit(solution)/shard_map/while/body/eval_jaxpr/vmap()/gather | solution.py:76
  328.4 35.7 %fusion.65 = (f32[16,1536,32]{1,0,2:T(8,128)S(1)}, f32[16,1536,32]{1,0,2:T(8,128)S(1)}, f32[16,1536,32]{1,0,2:T(8,128)S(1)}, f32[16,1536,32]{1,0,2:T(8,128)S(1)}) fusion(f32[16,1536,5]{1,2,0:T(8,128)S(1)} %copy.49, bf16[32,2,5,16,1536]{4,2,1,3,0:T(8,128)(2,1)} %gather_fusion, f32[16,1536,5]{1,2,0:T(8,128)S(1)} %copy.50), kind=kLoop, calls=%fused_computation.7.clone.1 | loop fusion | flops 36175872 | bytes 29294592 | tf_op jit(solution)/shard_map/while/body/eval_jaxpr/vmap(wcf,wcf->cf)/dot_general | solution.py:79
  364.1 3.0 subtract_bitcast_fusion.2
  367.2 8.8 %fusion.66 = f32[8,32,16,256]{3,2,1,0:T(8,128)} fusion(f32[8,32,16,256]{3,2,1,0:T(8,128)} %get-tuple-element.231, s32[]{:T(128)} %get-tuple-element.230, f32[3072,256]{1,0:T(8,128)} %get-tuple-element.243, f32[32,16,1536]{2,1,0:T(8,128)S(1)} %get-tuple-element.220, f32[32,16,1536]{2,1,0:T(8,128)} %get-tuple-element.221), kind=kOutput, calls=%fused_computation.19.clone.1 | convolution fusion | flops 4833411072 | bytes 9961984 | tf_op jit(solution)/shard_map/while/body/eval_jaxpr/dot_general | solution.py:93
  377.1 15.1 %gather_fusion = bf16[32,2,5,16,1536]{4,2,1,3,0:T(8,128)(2,1)} fusion(bf16[2,5,272,1536]{3,1,0,2:T(8,128)(2,1)} %get-tuple-element.241, s32[32]{0:T(128)S(1)} %shift-left_bitcast_fusion.2), kind=kCustom, calls=%fused_computation.clone.1 | custom fusion | bytes 31457792 | tf_op jit(solution)/shard_map/while/body/eval_jaxpr/vmap()/gather | solution.py:76
  393.0 35.7 %fusion.65 = (f32[16,1536,32]{1,0,2:T(8,128)S(1)}, f32[16,1536,32]{1,0,2:T(8,128)S(1)}, f32[16,1536,32]{1,0,2:T(8,128)S(1)}, f32[16,1536,32]{1,0,2:T(8,128)S(1)}) fusion(f32[16,1536,5]{1,2,0:T(8,128)S(1)} %copy.49, bf16[32,2,5,16,1536]{4,2,1,3,0:T(8,128)(2,1)} %gather_fusion, f32[16,1536,5]{1,2,0:T(8,128)S(1)} %copy.50), kind=kLoop, calls=%fused_computation.7.clone.1 | loop fusion | flops 36175872 | bytes 29294592 | tf_op jit(solution)/shard_map/while/body/eval_jaxpr/vmap(wcf,wcf->cf)/dot_general | solution.py:79
  428.7 3.0 subtract_bitcast_fusion.2
  431.7 8.7 %fusion.66 = f32[8,32,16,256]{3,2,1,0:T(8,128)} fusion(f32[8,32,16,256]{3,2,1,0:T(8,128)} %get-tuple-element.231, s32[]{:T(128)} %get-tuple-element.230, f32[3072,256]{1,0:T(8,128)} %get-tuple-element.243, f32[32,16,1536]{2,1,0:T(8,128)S(1)} %get-tuple-element.220, f32[32,16,1536]{2,1,0:T(8,128)} %get-tuple-element.221), kind=kOutput, calls=%fused_computation.19.clone.1 | convolution fusion | flops 4833411072 | bytes 9961984 | tf_op jit(solution)/shard_map/while/body/eval_jaxpr/dot_general | solution.py:93
  441.7 15.1 %gather_fusion = bf16[32,2,5,16,1536]{4,2,1,3,0:T(8,128)(2,1)} fusion(bf16[2,5,272,1536]{3,1,0,2:T(8,128)(2,1)} %get-tuple-element.241, s32[32]{0:T(128)S(1)} %shift-left_bitcast_fusion.2), kind=kCustom, calls=%fused_computation.clone.1 | custom fusion | bytes 31457792 | tf_op jit(solution)/shard_map/while/body/eval_jaxpr/vmap()/gather | solution.py:76
  457.5 35.7 %fusion.65 = (f32[16,1536,32]{1,0,2:T(8,128)S(1)}, f32[16,1536,32]{1,0,2:T(8,128)S(1)}, f32[16,1536,32]{1,0,2:T(8,128)S(1)}, f32[16,1536,32]{1,0,2:T(8,128)S(1)}) fusion(f32[16,1536,5]{1,2,0:T(8,128)S(1)} %copy.49, bf16[32,2,5,16,1536]{4,2,1,3,0:T(8,128)(2,1)} %gather_fusion, f32[16,1536,5]{1,2,0:T(8,128)S(1)} %copy.50), kind=kLoop, calls=%fused_computation.7.clone.1 | loop fusion | flops 36175872 | bytes 29294592 | tf_op jit(solution)/shard_map/while/body/eval_jaxpr/vmap(wcf,wcf->cf)/dot_general | solution.py:79
  493.2 3.0 subtract_bitcast_fusion.2
  496.3 8.7 %fusion.66 = f32[8,32,16,256]{3,2,1,0:T(8,128)} fusion(f32[8,32,16,256]{3,2,1,0:T(8,128)} %get-tuple-element.231, s32[]{:T(128)} %get-tuple-element.230, f32[3072,256]{1,0:T(8,128)} %get-tuple-element.243, f32[32,16,1536]{2,1,0:T(8,128)S(1)} %get-tuple-element.220, f32[32,16,1536]{2,1,0:T(8,128)} %get-tuple-element.221), kind=kOutput, calls=%fused_computation.19.clone.1 | convolution fusion | flops 4833411072 | bytes 9961984 | tf_op jit(solution)/shard_map/while/body/eval_jaxpr/dot_general | solution.py:93
  506.2 15.1 %gather_fusion = bf16[32,2,5,16,1536]{4,2,1,3,0:T(8,128)(2,1)} fusion(bf16[2,5,272,1536]{3,1,0,2:T(8,128)(2,1)} %get-tuple-element.241, s32[32]{0:T(128)S(1)} %shift-left_bitcast_fusion.2), kind=kCustom, calls=%fused_computation.clone.1 | custom fusion | bytes 31457792 | tf_op jit(solution)/shard_map/while/body/eval_jaxpr/vmap()/gather | solution.py:76
  522.1 35.7 %fusion.65 = (f32[16,1536,32]{1,0,2:T(8,128)S(1)}, f32[16,1536,32]{1,0,2:T(8,128)S(1)}, f32[16,1536,32]{1,0,2:T(8,128)S(1)}, f32[16,1536,32]{1,0,2:T(8,128)S(1)}) fusion(f32[16,1536,5]{1,2,0:T(8,128)S(1)} %copy.49, bf16[32,2,5,16,1536]{4,2,1,3,0:T(8,128)(2,1)} %gather_fusion, f32[16,1536,5]{1,2,0:T(8,128)S(1)} %copy.50), kind=kLoop, calls=%fused_computation.7.clone.1 | loop fusion | flops 36175872 | bytes 29294592 | tf_op jit(solution)/shard_map/while/body/eval_jaxpr/vmap(wcf,wcf->cf)/dot_general | solution.py:79
  557.8 3.0 subtract_bitcast_fusion.2
  560.8 8.7 %fusion.66 = f32[8,32,16,256]{3,2,1,0:T(8,128)} fusion(f32[8,32,16,256]{3,2,1,0:T(8,128)} %get-tuple-element.231, s32[]{:T(128)} %get-tuple-element.230, f32[3072,256]{1,0:T(8,128)} %get-tuple-element.243, f32[32,16,1536]{2,1,0:T(8,128)S(1)} %get-tuple-element.220, f32[32,16,1536]{2,1,0:T(8,128)} %get-tuple-element.221), kind=kOutput, calls=%fused_computation.19.clone.1 | convolution fusion | flops 4833411072 | bytes 9961984 | tf_op jit(solution)/shard_map/while/body/eval_jaxpr/dot_general | solution.py:93
  570.7 15.1 %gather_fusion = bf16[32,2,5,16,1536]{4,2,1,3,0:T(8,128)(2,1)} fusion(bf16[2,5,272,1536]{3,1,0,2:T(8,128)(2,1)} %get-tuple-element.241, s32[32]{0:T(128)S(1)} %shift-left_bitcast_fusion.2), kind=kCustom, calls=%fused_computation.clone.1 | custom fusion | bytes 31457792 | tf_op jit(solution)/shard_map/while/body/eval_jaxpr/vmap()/gather | solution.py:76
  586.6 35.7 %fusion.65 = (f32[16,1536,32]{1,0,2:T(8,128)S(1)}, f32[16,1536,32]{1,0,2:T(8,128)S(1)}, f32[16,1536,32]{1,0,2:T(8,128)S(1)}, f32[16,1536,32]{1,0,2:T(8,128)S(1)}) fusion(f32[16,1536,5]{1,2,0:T(8,128)S(1)} %copy.49, bf16[32,2,5,16,1536]{4,2,1,3,0:T(8,128)(2,1)} %gather_fusion, f32[16,1536,5]{1,2,0:T(8,128)S(1)} %copy.50), kind=kLoop, calls=%fused_computation.7.clone.1 | loop fusion | flops 36175872 | bytes 29294592 | tf_op jit(solution)/shard_map/while/body/eval_jaxpr/vmap(wcf,wcf->cf)/dot_general | solution.py:79
  622.3 3.0 subtract_bitcast_fusion.2
  625.3 8.8 %fusion.66 = f32[8,32,16,256]{3,2,1,0:T(8,128)} fusion(f32[8,32,16,256]{3,2,1,0:T(8,128)} %get-tuple-element.231, s32[]{:T(128)} %get-tuple-element.230, f32[3072,256]{1,0:T(8,128)} %get-tuple-element.243, f32[32,16,1536]{2,1,0:T(8,128)S(1)} %get-tuple-element.220, f32[32,16,1536]{2,1,0:T(8,128)} %get-tuple-element.221), kind=kOutput, calls=%fused_computation.19.clone.1 | convolution fusion | flops 4833411072 | bytes 9961984 | tf_op jit(solution)/shard_map/while/body/eval_jaxpr/dot_general | solution.py:93
  635.3 15.1 %gather_fusion = bf16[32,2,5,16,1536]{4,2,1,3,0:T(8,128)(2,1)} fusion(bf16[2,5,272,1536]{3,1,0,2:T(8,128)(2,1)} %get-tuple-element.241, s32[32]{0:T(128)S(1)} %shift-left_bitcast_fusion.2), kind=kCustom, calls=%fused_computation.clone.1 | custom fusion | bytes 31457792 | tf_op jit(solution)/shard_map/while/body/eval_jaxpr/vmap()/gather | solution.py:76
  651.2 35.7 %fusion.65 = (f32[16,1536,32]{1,0,2:T(8,128)S(1)}, f32[16,1536,32]{1,0,2:T(8,128)S(1)}, f32[16,1536,32]{1,0,2:T(8,128)S(1)}, f32[16,1536,32]{1,0,2:T(8,128)S(1)}) fusion(f32[16,1536,5]{1,2,0:T(8,128)S(1)} %copy.49, bf16[32,2,5,16,1536]{4,2,1,3,0:T(8,128)(2,1)} %gather_fusion, f32[16,1536,5]{1,2,0:T(8,128)S(1)} %copy.50), kind=kLoop, calls=%fused_computation.7.clone.1 | loop fusion | flops 36175872 | bytes 29294592 | tf_op jit(solution)/shard_map/while/body/eval_jaxpr/vmap(wcf,wcf->cf)/dot_general | solution.py:79
  686.9 3.0 subtract_bitcast_fusion.2
  689.9 8.7 %fusion.66 = f32[8,32,16,256]{3,2,1,0:T(8,128)} fusion(f32[8,32,16,256]{3,2,1,0:T(8,128)} %get-tuple-element.231, s32[]{:T(128)} %get-tuple-element.230, f32[3072,256]{1,0:T(8,128)} %get-tuple-element.243, f32[32,16,1536]{2,1,0:T(8,128)S(1)} %get-tuple-element.220, f32[32,16,1536]{2,1,0:T(8,128)} %get-tuple-element.221), kind=kOutput, calls=%fused_computation.19.clone.1 | convolution fusion | flops 4833411072 | bytes 9961984 | tf_op jit(solution)/shard_map/while/body/eval_jaxpr/dot_general | solution.py:93
  698.8 12.3 %fusion.24 = f32[256,16,256]{0,2,1:T(8,128)} fusion(f32[256,16,256]{2,1,0:T(8,128)} %bitcast.87, f32[16,256]{1,0:T(8,128)} %convert_multiply_fusion.6, s32[16,256]{1,0:T(8,128)S(1)} %copy-done), kind=kOutput, calls=%fused_computation.33 | convolution fusion | flops 3223322624 | bytes 8421376 | tf_op jit(solution)/shard_map/cjo,oct->jct/dot_general | solution.py:110
  711.1 5.5 copy.10
  716.6 84.1 %reduce-scatter.2.cloned.1.call-done = f32[64,16,256]{2,1,0:T(8,128)} async-done(((f32[256,16,256]{2,1,0:T(8,128)}), f32[64,16,256]{2,1,0:T(8,128)}) %reduce-scatter.2.cloned.1.call-update) | async-done | bytes 1048592 | tf_op jit(solution)/shard_map/reduce_scatter | solution.py:109
  (118 shorter events, 14.3 us)
Async XLA Ops:
  6.5 794.2 %reduce-scatter.2.cloned.1.call-start = ((), (), s32[]{:S(2)}) async-start(), calls=%async_computation.1 | async-start | bytes 5242880 | tf_op jit(solution)/shard_map/reduce_scatter | solution.py:109
  8.6 33.8 %copy-start.1 = (s32[16,256]{1,0:T(8,128)S(1)}, s32[16,256]{1,0:T(8,128)}, u32[]{:S(2)}) copy-start(s32[16,256]{1,0:T(8,128)} %param.7) | copy-start | bytes 49156
  8.6 34.4 %copy-start.2 = (s32[16,256]{1,0:T(8,128)S(1)}, s32[16,256]{1,0:T(8,128)}, u32[]{:S(2)}) copy-start(s32[16,256]{1,0:T(8,128)} %param.8) | copy-start | bytes 49156
  12.8 47.2 %collective-permute-start = (bf16[2,5,16,1536]{3,2,1,0:T(8,128)(2,1)S(1)}, bf16[2,5,16,1536]{3,2,1,0:T(8,128)(2,1)S(1)}, u32[]{:S(2)}, u32[]{:S(2)}) collective-permute-start(bf16[2,5,16,1536]{3,2,1,0:T(8,128)(2,1)S(1)} %pad_maximum_fusion), channel_id=1, source_target_pairs={{0,32},{4,36},{8,40},{12,44},{16,48},{20,52},{24,56},{28,60},{32,6... | collective-permute-start | bytes 1474568 | tf_op jit(solution)/shard_map/ppermute | solution.py:20
  18.5 45.9 %collective-permute-start.1 = (bf16[2,5,16,1536]{3,2,1,0:T(8,128)(2,1)S(1)}, bf16[2,5,16,1536]{3,2,1,0:T(8,128)(2,1)S(1)}, u32[]{:S(2)}, u32[]{:S(2)}) collective-permute-start(bf16[2,5,16,1536]{3,2,1,0:T(8,128)(2,1)S(1)} %pad_maximum_fusion), channel_id=1, source_target_pairs={{0,28},{4,32},{8,36},{12,40},{16,44},{20,48},{24,52},{28,56},{32,6... | collective-permute-start | bytes 1474568 | tf_op jit(solution)/shard_map/ppermute | solution.py:20
  23.0 43.1 %collective-permute-start.2 = (bf16[2,5,16,1536]{3,2,1,0:T(8,128)(2,1)S(1)}, bf16[2,5,16,1536]{3,2,1,0:T(8,128)(2,1)S(1)}, u32[]{:S(2)}, u32[]{:S(2)}) collective-permute-start(bf16[2,5,16,1536]{3,2,1,0:T(8,128)(2,1)S(1)} %pad_maximum_fusion), channel_id=1, source_target_pairs={{0,24},{4,28},{8,32},{12,36},{16,40},{20,44},{24,48},{28,52},{32,5... | collective-permute-start | bytes 1474568 | tf_op jit(solution)/shard_map/ppermute | solution.py:20
  27.5 41.5 %collective-permute-start.3 = (bf16[2,5,16,1536]{3,2,1,0:T(8,128)(2,1)S(1)}, bf16[2,5,16,1536]{3,2,1,0:T(8,128)(2,1)S(1)}, u32[]{:S(2)}, u32[]{:S(2)}) collective-permute-start(bf16[2,5,16,1536]{3,2,1,0:T(8,128)(2,1)S(1)} %pad_maximum_fusion), channel_id=1, source_target_pairs={{0,20},{4,24},{8,28},{12,32},{16,36},{20,40},{24,44},{28,48},{32,5... | collective-permute-start | bytes 1474568 | tf_op jit(solution)/shard_map/ppermute | solution.py:20
  31.0 71.1 %collective-permute-start.4 = (bf16[2,5,16,1536]{3,2,1,0:T(8,128)(2,1)S(1)}, bf16[2,5,16,1536]{3,2,1,0:T(8,128)(2,1)S(1)}, u32[]{:S(2)}, u32[]{:S(2)}) collective-permute-start(bf16[2,5,16,1536]{3,2,1,0:T(8,128)(2,1)S(1)} %pad_maximum_fusion), channel_id=1, source_target_pairs={{0,16},{4,20},{8,24},{12,28},{16,32},{20,36},{24,40},{28,44},{32,4... | collective-permute-start | bytes 1474568 | tf_op jit(solution)/shard_map/ppermute | solution.py:20
  60.0 43.5 %collective-permute-start.5 = (bf16[2,5,16,1536]{3,2,1,0:T(8,128)(2,1)S(1)}, bf16[2,5,16,1536]{3,2,1,0:T(8,128)(2,1)S(1)}, u32[]{:S(2)}, u32[]{:S(2)}) collective-permute-start(bf16[2,5,16,1536]{3,2,1,0:T(8,128)(2,1)S(1)} %pad_maximum_fusion), channel_id=1, source_target_pairs={{0,12},{4,16},{8,20},{12,24},{16,28},{20,32},{24,36},{28,40},{32,4... | collective-permute-start | bytes 1474568 | tf_op jit(solution)/shard_map/ppermute | solution.py:20
  64.4 40.4 %collective-permute-start.6 = (bf16[2,5,16,1536]{3,2,1,0:T(8,128)(2,1)S(1)}, bf16[2,5,16,1536]{3,2,1,0:T(8,128)(2,1)S(1)}, u32[]{:S(2)}, u32[]{:S(2)}) collective-permute-start(bf16[2,5,16,1536]{3,2,1,0:T(8,128)(2,1)S(1)} %pad_maximum_fusion), channel_id=1, source_target_pairs={{0,8},{4,12},{8,16},{12,20},{16,24},{20,28},{24,32},{28,36},{32,40... | collective-permute-start | bytes 1474568 | tf_op jit(solution)/shard_map/ppermute | solution.py:20
  66.1 40.0 %collective-permute-start.7 = (bf16[2,5,16,1536]{3,2,1,0:T(8,128)(2,1)S(1)}, bf16[2,5,16,1536]{3,2,1,0:T(8,128)(2,1)S(1)}, u32[]{:S(2)}, u32[]{:S(2)}) collective-permute-start(bf16[2,5,16,1536]{3,2,1,0:T(8,128)(2,1)S(1)} %pad_maximum_fusion), channel_id=1, source_target_pairs={{0,4},{4,8},{8,12},{12,16},{16,20},{20,24},{24,28},{28,32},{32,36}... | collective-permute-start | bytes 1474568 | tf_op jit(solution)/shard_map/ppermute | solution.py:20
  69.0 38.5 %collective-permute-start.8 = (bf16[2,5,16,1536]{3,2,1,0:T(8,128)(2,1)S(1)}, bf16[2,5,16,1536]{3,2,1,0:T(8,128)(2,1)S(1)}, u32[]{:S(2)}, u32[]{:S(2)}) collective-permute-start(bf16[2,5,16,1536]{3,2,1,0:T(8,128)(2,1)S(1)} %pad_maximum_fusion), channel_id=1, source_target_pairs={{4,0},{8,4},{12,8},{16,12},{20,16},{24,20},{28,24},{32,28},{36,32}... | collective-permute-start | bytes 1474568 | tf_op jit(solution)/shard_map/ppermute | solution.py:20
  102.1 14.6 %collective-permute-start.9 = (bf16[2,5,16,1536]{3,2,1,0:T(8,128)(2,1)S(1)}, bf16[2,5,16,1536]{3,2,1,0:T(8,128)(2,1)S(1)}, u32[]{:S(2)}, u32[]{:S(2)}) collective-permute-start(bf16[2,5,16,1536]{3,2,1,0:T(8,128)(2,1)S(1)} %pad_maximum_fusion), channel_id=1, source_target_pairs={{8,0},{12,4},{16,8},{20,12},{24,16},{28,20},{32,24},{36,28},{40,32... | collective-permute-start | bytes 1474568 | tf_op jit(solution)/shard_map/ppermute | solution.py:20
  103.5 25.7 %collective-permute-start.10 = (bf16[2,5,16,1536]{3,2,1,0:T(8,128)(2,1)S(1)}, bf16[2,5,16,1536]{3,2,1,0:T(8,128)(2,1)S(1)}, u32[]{:S(2)}, u32[]{:S(2)}) collective-permute-start(bf16[2,5,16,1536]{3,2,1,0:T(8,128)(2,1)S(1)} %pad_maximum_fusion), channel_id=1, source_target_pairs={{12,0},{16,4},{20,8},{24,12},{28,16},{32,20},{36,24},{40,28},{44,3... | collective-permute-start | bytes 1474568 | tf_op jit(solution)/shard_map/ppermute | solution.py:20
  104.8 27.3 %collective-permute-start.11 = (bf16[2,5,16,1536]{3,2,1,0:T(8,128)(2,1)S(1)}, bf16[2,5,16,1536]{3,2,1,0:T(8,128)(2,1)S(1)}, u32[]{:S(2)}, u32[]{:S(2)}) collective-permute-start(bf16[2,5,16,1536]{3,2,1,0:T(8,128)(2,1)S(1)} %pad_maximum_fusion), channel_id=1, source_target_pairs={{16,0},{20,4},{24,8},{28,12},{32,16},{36,20},{40,24},{44,28},{48,3... | collective-permute-start | bytes 1474568 | tf_op jit(solution)/shard_map/ppermute | solution.py:20
  106.2 26.0 %collective-permute-start.12 = (bf16[2,5,16,1536]{3,2,1,0:T(8,128)(2,1)S(1)}, bf16[2,5,16,1536]{3,2,1,0:T(8,128)(2,1)S(1)}, u32[]{:S(2)}, u32[]{:S(2)}) collective-permute-start(bf16[2,5,16,1536]{3,2,1,0:T(8,128)(2,1)S(1)} %pad_maximum_fusion), channel_id=1, source_target_pairs={{20,0},{24,4},{28,8},{32,12},{36,16},{40,20},{44,24},{48,28},{52,3... | collective-permute-start | bytes 1474568 | tf_op jit(solution)/shard_map/ppermute | solution.py:20
  107.6 32.2 %collective-permute-start.13 = (bf16[2,5,16,1536]{3,2,1,0:T(8,128)(2,1)S(1)}, bf16[2,5,16,1536]{3,2,1,0:T(8,128)(2,1)S(1)}, u32[]{:S(2)}, u32[]{:S(2)}) collective-permute-start(bf16[2,5,16,1536]{3,2,1,0:T(8,128)(2,1)S(1)} %pad_maximum_fusion), channel_id=1, source_target_pairs={{24,0},{28,4},{32,8},{36,12},{40,16},{44,20},{48,24},{52,28},{56,3... | collective-permute-start | bytes 1474568 | tf_op jit(solution)/shard_map/ppermute | solution.py:20
  116.7 35.4 %collective-permute-start.14 = (bf16[2,5,16,1536]{3,2,1,0:T(8,128)(2,1)S(1)}, bf16[2,5,16,1536]{3,2,1,0:T(8,128)(2,1)S(1)}, u32[]{:S(2)}, u32[]{:S(2)}) collective-permute-start(bf16[2,5,16,1536]{3,2,1,0:T(8,128)(2,1)S(1)} %pad_maximum_fusion), channel_id=1, source_target_pairs={{28,0},{32,4},{36,8},{40,12},{44,16},{48,20},{52,24},{56,28},{60,3... | collective-permute-start | bytes 1474568 | tf_op jit(solution)/shard_map/ppermute | solution.py:20
  129.2 23.0 %collective-permute-start.15 = (bf16[2,5,16,1536]{3,2,1,0:T(8,128)(2,1)S(1)}, bf16[2,5,16,1536]{3,2,1,0:T(8,128)(2,1)S(1)}, u32[]{:S(2)}, u32[]{:S(2)}) collective-permute-start(bf16[2,5,16,1536]{3,2,1,0:T(8,128)(2,1)S(1)} %pad_maximum_fusion), channel_id=1, source_target_pairs={{32,0},{36,4},{40,8},{44,12},{48,16},{52,20},{56,24},{60,28},{64,3... | collective-permute-start | bytes 1474568 | tf_op jit(solution)/shard_map/ppermute | solution.py:20
  182.3 516.5 %copy-start = (s32[16,256]{1,0:T(8,128)S(1)}, s32[16,256]{1,0:T(8,128)}, u32[]{:S(2)}) copy-start(s32[16,256]{1,0:T(8,128)} %select_clamp_fusion) | copy-start | bytes 49156
  182.3 1.2 copy-start.3
  238.1 8.7 %copy-start.4 = (s32[8]{0:T(128)S(1)}, s32[8]{0:T(128)}, u32[]{:S(2)}) copy-start(s32[8]{0:T(128)} %copy-done.3) | copy-start | bytes 100 | tf_op jit(solution)/shard_map/while
  246.9 1.2 copy-start.3
  302.7 8.7 %copy-start.4 = (s32[8]{0:T(128)S(1)}, s32[8]{0:T(128)}, u32[]{:S(2)}) copy-start(s32[8]{0:T(128)} %copy-done.3) | copy-start | bytes 100 | tf_op jit(solution)/shard_map/while
  311.4 1.2 copy-start.3
  367.2 8.8 %copy-start.4 = (s32[8]{0:T(128)S(1)}, s32[8]{0:T(128)}, u32[]{:S(2)}) copy-start(s32[8]{0:T(128)} %copy-done.3) | copy-start | bytes 100 | tf_op jit(solution)/shard_map/while
  375.9 1.2 copy-start.3
  431.7 8.7 %copy-start.4 = (s32[8]{0:T(128)S(1)}, s32[8]{0:T(128)}, u32[]{:S(2)}) copy-start(s32[8]{0:T(128)} %copy-done.3) | copy-start | bytes 100 | tf_op jit(solution)/shard_map/while
  440.5 1.2 copy-start.3
  496.3 8.7 %copy-start.4 = (s32[8]{0:T(128)S(1)}, s32[8]{0:T(128)}, u32[]{:S(2)}) copy-start(s32[8]{0:T(128)} %copy-done.3) | copy-start | bytes 100 | tf_op jit(solution)/shard_map/while
  505.0 1.2 copy-start.3
  560.8 8.7 %copy-start.4 = (s32[8]{0:T(128)S(1)}, s32[8]{0:T(128)}, u32[]{:S(2)}) copy-start(s32[8]{0:T(128)} %copy-done.3) | copy-start | bytes 100 | tf_op jit(solution)/shard_map/while
  569.5 1.2 copy-start.3
  625.3 8.8 %copy-start.4 = (s32[8]{0:T(128)S(1)}, s32[8]{0:T(128)}, u32[]{:S(2)}) copy-start(s32[8]{0:T(128)} %copy-done.3) | copy-start | bytes 100 | tf_op jit(solution)/shard_map/while
  634.1 1.2 copy-start.3
  689.9 8.7 %copy-start.4 = (s32[8]{0:T(128)S(1)}, s32[8]{0:T(128)}, u32[]{:S(2)}) copy-start(s32[8]{0:T(128)} %copy-done.3) | copy-start | bytes 100 | tf_op jit(solution)/shard_map/while
Sparse Core Ops, SparseCore 0:
  716.7 83.9 reduce-scatter.1
where the time goes:
time: 817 us; the launch traced here: 808 us
  other arithmetic  327 us (40%)
  waiting for transfers between devices  172 us (21%)
  local copies, waits for them, and re-layouts  167 us (20%)
  matrix products  82.2 us (10%)
  starting transfers between devices  40.6 us (5%)
  between operations  14 us (2%)
    dot_general x8, other arithmetic, one_offset(): jnp.einsum('wcf,wcf->cf', whitened[1], partner_rows[1], preferred_element...  286 us
    gather x8, local copies, waits for them, and re-layouts, one_offset(): lax.dynamic_slice_in_dim(extended, shift_by + reach_span, channels, 2)  121 us
    ppermute x16, waiting for transfers between devices, passed_along(): lax.ppermute(value, axis, [(source, source + steps) for source in range(f...  88.3 us
    reduce_scatter x1, waiting for transfers between devices, on_device(): lax.psum_scatter(jnp.einsum('cjo,oct->jct', picker, by_offset, precision=...  84.1 us
    dot_general x8, matrix products, offset_block(): jnp.dot(joined, basis, precision=lax.Precision.HIGHEST, preferred_element...  69.9 us
    ppermute x16, starting transfers between devices, passed_along(): lax.ppermute(value, axis, [(source, source + steps) for source in range(f...  40.6 us
    while x1, local copies, waits for them, and re-layouts, on_device(): lax.map(offset_block, jnp.arange(slots // group, dtype=jnp.int32))  30.1 us
    sub x8, other arithmetic, one_offset(): jnp.einsum('wcf,wcf->cf', whitened[1], partner_rows[0], preferred_element...  24.3 us
  transfers between devices with their start and end apart: 17, of which 8 were waited for; matrix products, arithmetic and copies ran while one was open for 1% of the time, Pallas kernels for 0%

commit v1 on v0

v1 whole, which is shorter than its diff:
```python
import math

import jax
import jax.numpy as jnp
import numpy as np
from jax import lax
from jax.experimental import pallas as pl
from jax.experimental.pallas import tpu as pltpu
from jax.sharding import PartitionSpec as P

LAGS = 256
SMOOTH = 8
FLO = 64
NSAMP = 6000
water_level = 0.1

MESH = pl.DeviceIdType.MESH
BLOCKS = 7
TILE = 128
SUB = 16
QUAD = 64
QUAD_LANES = 640
CHUNK = 256
CHUNK_LANES = CHUNK // QUAD * QUAD_LANES


def bin_order():
    main = np.zeros((8 * TILE, 8 * TILE), np.float32)
    part, f = np.meshgrid(np.arange(8), np.arange(TILE), indexing="ij")
    main[part * TILE + f, (f // SUB) * TILE + part * SUB + f % SUB] = 1.0
    rest = np.zeros((2 * TILE, 2 * TILE), np.float32)
    part, f = np.meshgrid(np.arange(2), np.arange(TILE), indexing="ij")
    rest[part * TILE + f, (f // QUAD) * TILE + part * QUAD + f % QUAD] = 1.0
    return main.astype(jnp.bfloat16), rest.astype(jnp.bfloat16)


def lag_tables(bins):
    steps = np.mod((FLO + np.arange(bins))[:, None] * (np.arange(LAGS) - LAGS // 2)[None, :], NSAMP)
    angles = steps.astype(np.float64) * (2.0 * math.pi / NSAMP)
    shape = (bins // CHUNK, CHUNK, LAGS)
    return (
        np.cos(angles).astype(np.float32).reshape(shape).astype(jnp.bfloat16),
        np.sin(angles).astype(np.float32).reshape(shape).astype(jnp.bfloat16),
    )


def whiten_kernel(spectra_ref, live_ref, main_ref, rest_ref, x_ref, y_ref, held):
    windows, channels, bins = spectra_ref.shape[1:]
    tiles = bins // TILE
    position = lax.broadcasted_iota(jnp.int32, (1, bins), 1)
    count = (jnp.minimum(position + SMOOTH, bins - 1) - jnp.maximum(position - SMOOTH, 0) + 1).astype(jnp.float32)
    live = live_ref[...]
    pad = jnp.zeros((channels, TILE), jnp.float32)
    for window in range(windows):
        real_part = spectra_ref[0, window].astype(jnp.float32)
        imag_part = spectra_ref[1, window].astype(jnp.float32)
        magnitude = jnp.sqrt(real_part * real_part + imag_part * imag_part)
        band_mean = jnp.sum(magnitude, axis=1, keepdims=True) * (1.0 / bins)
        padded = jnp.concatenate([magnitude, pad], axis=1)
        width = bins + TILE
        total = padded
        for step in (1, 2, 4, 8):
            total = total + pltpu.roll(total, step, 1)
        around = pltpu.roll(total, width - SMOOTH, 1) + pltpu.roll(padded, SMOOTH, 1)
        divisor = around[:, :bins] / count + water_level * band_mean + 1e-06
        white_real = (real_part / divisor * live).astype(jnp.bfloat16)
        white_imag = (imag_part / divisor * live).astype(jnp.bfloat16)
        minus_real = -white_real
        for tile in range(tiles):
            rows = slice(tile * channels, (tile + 1) * channels)
            lanes = slice(tile * TILE, (tile + 1) * TILE)
            first = slice(2 * window * TILE, (2 * window + 1) * TILE)
            second = slice((2 * window + 1) * TILE, (2 * window + 2) * TILE)
            held[0, rows, first] = white_real[:, lanes]
            held[0, rows, second] = white_imag[:, lanes]
            held[1, rows, first] = white_imag[:, lanes]
            held[1, rows, second] = minus_real[:, lanes]
    for which, out_ref in ((0, x_ref), (1, y_ref)):
        main = jnp.dot(held[which, :, : 8 * TILE], main_ref[...], preferred_element_type=jnp.float32)
        rest = jnp.dot(held[which, :, 8 * TILE :], rest_ref[...], preferred_element_type=jnp.float32)
        main = main.astype(jnp.bfloat16)
        rest = rest.astype(jnp.bfloat16)
        for tile in range(tiles):
            rows = slice(tile * channels, (tile + 1) * channels)
            for half in range(2):
                quad = tile * 2 + half
                chunk, start = quad // (CHUNK // QUAD), quad % (CHUNK // QUAD) * QUAD_LANES
                out_ref[chunk, :, start : start + 4 * TILE] = main[rows, half * 4 * TILE : (half + 1) * 4 * TILE]
                out_ref[chunk, :, start + 4 * TILE : start + QUAD_LANES] = rest[rows, half * TILE : (half + 1) * TILE]


def stack_kernel(
    x_ref, y_ref, cos_ref, sin_ref, rel_ref, out_ref,
    around, cross, even, odd, ahead, back_out, back_in, picked, from_core, to_far, from_far,
    halo_send, halo_recv, back_send, back_recv, core_send, core_recv, far_send, far_recv,
):
    chunks, channels = x_ref.shape[:2]
    span = around.shape[1]
    count = lax.axis_size("chan")
    me = lax.axis_index("chan")
    win = lax.axis_index("win")
    core = lax.rem(win, 2)
    far = win // 2
    other_core = win + 1 - 2 * core
    other_far = lax.rem(win + 2, 4)

    def above(distance):
        return lax.rem(me + distance, count)

    def below(distance):
        return lax.rem(me + count - distance, count)

    barrier = pltpu.get_barrier_semaphore()
    for distance in range(1, BLOCKS + 1):
        for chan in (above(distance), below(distance)):
            pl.semaphore_signal(barrier, inc=1, device_id={"chan": chan, "win": win}, device_id_type=MESH)
    for partner in (other_core, other_far):
        pl.semaphore_signal(barrier, inc=1, device_id={"chan": me, "win": partner}, device_id_type=MESH)
    pl.semaphore_wait(barrier, 2 * BLOCKS + 2)

    def halo(chunk, distance):
        return pltpu.make_async_remote_copy(
            src_ref=x_ref.at[chunk],
            dst_ref=around.at[chunk, pl.ds(distance * channels, channels), :],
            send_sem=halo_send.at[chunk, distance - 1],
            recv_sem=halo_recv.at[chunk, distance - 1],
            device_id={"chan": below(distance), "win": win},
            device_id_type=MESH,
        )

    for chunk in range(chunks):
        for distance in range(1, BLOCKS + 1):
            halo(chunk, distance).start()
    for chunk in range(chunks):
        around[chunk, :channels, :] = x_ref[chunk]
    even[...] = jnp.zeros_like(even)
    odd[...] = jnp.zeros_like(odd)

    row = lax.broadcasted_iota(jnp.int32, (SUB, TILE), 0)
    lane = lax.broadcasted_iota(jnp.int32, (SUB, TILE), 1)
    masks = []
    for group in range(QUAD // SUB):
        main = (lane % SUB == row).astype(jnp.float32)
        rest = (lane % QUAD == group * SUB + row).astype(jnp.float32)
        masks.append(jnp.concatenate([main, rest], axis=1).astype(jnp.bfloat16))

    def one_chunk(chunk, _):
        for distance in range(1, BLOCKS + 1):
            halo(chunk, distance).wait_recv()

        def one_quad(quad, _):
            start = pl.multiple_of(quad * QUAD_LANES, TILE)

            def tiles(ref, group):
                first = ref[chunk, :, pl.ds(pl.multiple_of(start + group * TILE, TILE), TILE)]
                last = ref[chunk, :, pl.ds(pl.multiple_of(start + 4 * TILE, TILE), TILE)]
                return jnp.concatenate([first, last], axis=1)

            for group in range(QUAD // SUB):
                partners = tiles(around, group)
                for part, ref in ((0, x_ref), (1, y_ref)):
                    own = tiles(ref, group)
                    spread = (own[:, None, :] * masks[group][None, :, :]).reshape(channels * SUB, 2 * TILE)
                    product = lax.dot_general(
                        spread, partners, (((1,), (1,)), ((), ())), preferred_element_type=jnp.float32
                    )
                    first_bin = pl.multiple_of(quad * QUAD + group * SUB, SUB)
                    cross[part, :, pl.ds(first_bin, SUB), :] = product.astype(jnp.bfloat16).reshape(channels, SUB, span)
            return 0

        lax.fori_loop(0, CHUNK // QUAD, one_quad, 0)

        def one_channel(channel, _):
            for part, table, total in ((0, cos_ref, even), (1, sin_ref, odd)):
                total[channel] += lax.dot_general(
                    cross[part, channel], table[chunk], (((0,), (0,)), ((), ())), preferred_element_type=jnp.float32
                )
            return 0

        lax.fori_loop(0, channels, one_channel, 0)
        return 0

    lax.fori_loop(0, chunks, one_chunk, 0)

    def lags_of(channel, _):
        cos_sum = even[channel]
        sin_sum = odd[channel]
        ahead[channel] = (cos_sum - sin_sum).astype(jnp.bfloat16)
        mirrored = (cos_sum + sin_sum).astype(jnp.bfloat16)
        for distance in range(1, BLOCKS + 1):
            back_out[distance - 1, channel] = mirrored[distance * channels : (distance + 1) * channels]
        return 0

    lax.fori_loop(0, channels, lags_of, 0)

    def back(distance):
        return pltpu.make_async_remote_copy(
            src_ref=back_out.at[distance - 1],
            dst_ref=back_in.at[distance - 1],
            send_sem=back_send.at[distance - 1],
            recv_sem=back_recv.at[distance - 1],
            device_id={"chan": above(distance), "win": win},
            device_id_type=MESH,
        )

    for distance in range(1, BLOCKS + 1):
        back(distance).start()
    for distance in range(1, BLOCKS + 1):
        back(distance).wait_recv()

    slots = rel_ref.shape[1]

    def pick(channel, _):
        target = rel_ref[channel]
        lanes = lax.broadcasted_iota(jnp.int32, (slots, span), 1)
        chosen = (lanes == target).astype(jnp.float32).astype(jnp.bfloat16)
        total = jnp.dot(chosen, ahead[channel], preferred_element_type=jnp.float32)
        lanes = lax.broadcasted_iota(jnp.int32, (slots, channels * channels), 1)
        for distance in range(1, BLOCKS + 1):
            place = (target + distance * channels) * channels + channel
            chosen = (lanes == place).astype(jnp.float32).astype(jnp.bfloat16)
            rows = back_in[distance - 1].reshape(channels * channels, LAGS)
            total += jnp.dot(chosen, rows, preferred_element_type=jnp.float32)
        picked[channel] = total.astype(jnp.bfloat16)
        return 0

    lax.fori_loop(0, channels, pick, 0)

    share = slots // 4

    def slots_of(owner):
        return pl.ds(pl.multiple_of(owner * share, share), share)

    def to_core(half):
        return pltpu.make_async_remote_copy(
            src_ref=picked.at[:, slots_of(2 * half + 1 - core), :],
            dst_ref=from_core.at[half],
            send_sem=core_send.at[half],
            recv_sem=core_recv.at[half],
            device_id={"chan": me, "win": other_core},
            device_id_type=MESH,
        )

    for half in range(2):
        to_core(half).start()
    for half in range(2):
        to_core(half).wait_recv()

    def far_sum(channel, _):
        mine = picked[channel, slots_of(other_far), :].astype(jnp.float32)
        to_far[channel] = (mine + from_core[1 - far, channel].astype(jnp.float32)).astype(jnp.bfloat16)
        return 0

    lax.fori_loop(0, channels, far_sum, 0)
    away = pltpu.make_async_remote_copy(
        src_ref=to_far,
        dst_ref=from_far,
        send_sem=far_send,
        recv_sem=far_recv,
        device_id={"chan": me, "win": other_far},
        device_id_type=MESH,
    )
    away.start()
    away.wait_recv()

    def last_sum(channel, _):
        mine = picked[channel, slots_of(win), :].astype(jnp.float32)
        out_ref[channel] = (
            mine + from_core[far, channel].astype(jnp.float32) + from_far[channel].astype(jnp.float32)
        )
        return 0

    lax.fori_loop(0, channels, last_sum, 0)

    for chunk in range(chunks):
        for distance in range(1, BLOCKS + 1):
            halo(chunk, distance).wait_send()
    for distance in range(1, BLOCKS + 1):
        back(distance).wait_send()
    for half in range(2):
        to_core(half).wait_send()
    away.wait_send()


def on_device(spectra, partners, pair_mask, gap_flags):
    _, windows, channels, bins = spectra.shape
    slots = partners.shape[1]
    chunks = bins // CHUNK
    span = (BLOCKS + 1) * channels
    share = slots // 4
    bf16 = jnp.bfloat16
    whole = pl.BlockSpec(memory_space=pltpu.VMEM)
    main, rest = bin_order()
    cos_table, sin_table = lag_tables(bins)
    live = (gap_flags == 0).astype(jnp.float32)[:, None]
    own = jax.ShapeDtypeStruct((chunks, channels, CHUNK_LANES), bf16)
    x, y = pl.pallas_call(
        whiten_kernel,
        out_shape=(own, own),
        in_specs=[whole] * 4,
        out_specs=(whole, whole),
        scratch_shapes=[pltpu.VMEM((2, bins // TILE * channels, 2 * windows * TILE), bf16)],
        compiler_params=pltpu.CompilerParams(vmem_limit_bytes=40 * 2**20),
        name="whiten",
    )(spectra, live, main, rest)

    first = lax.axis_index("chan") * channels
    rel = jnp.where(pair_mask > 0, partners - first, -(2**20))[:, :, None]
    stacked = pl.pallas_call(
        stack_kernel,
        out_shape=jax.ShapeDtypeStruct((channels, share, LAGS), jnp.float32),
        in_specs=[whole] * 5,
        out_specs=whole,
        scratch_shapes=[
            pltpu.VMEM((chunks, span, CHUNK_LANES), bf16),
            pltpu.VMEM((2, channels, CHUNK, span), bf16),
            pltpu.VMEM((channels, span, LAGS), jnp.float32),
            pltpu.VMEM((channels, span, LAGS), jnp.float32),
            pltpu.VMEM((channels, span, LAGS), bf16),
            pltpu.VMEM((BLOCKS, channels, channels, LAGS), bf16),
            pltpu.VMEM((BLOCKS, channels, channels, LAGS), bf16),
            pltpu.VMEM((channels, slots, LAGS), bf16),
            pltpu.VMEM((2, channels, share, LAGS), bf16),
            pltpu.VMEM((channels, share, LAGS), bf16),
            pltpu.VMEM((channels, share, LAGS), bf16),
            pltpu.SemaphoreType.DMA((chunks, BLOCKS)),
            pltpu.SemaphoreType.DMA((chunks, BLOCKS)),
            pltpu.SemaphoreType.DMA((BLOCKS,)),
            pltpu.SemaphoreType.DMA((BLOCKS,)),
            pltpu.SemaphoreType.DMA((2,)),
            pltpu.SemaphoreType.DMA((2,)),
            pltpu.SemaphoreType.DMA,
            pltpu.SemaphoreType.DMA,
        ],
        compiler_params=pltpu.CompilerParams(
            collective_id=0, has_side_effects=True, vmem_limit_bytes=56 * 2**20
        ),
        name="stack",
    )(x, y, cos_table, sin_table, rel)
    scale = 1.0 / math.sqrt(windows * lax.axis_size("win") * bins)
    return jnp.transpose(stacked, (1, 0, 2)) * scale


def solution(mesh):
    placed = (P(None, "win", "chan", None), P("chan", None), P("chan", None), P("chan"))
    return jax.shard_map(
        on_device, mesh=mesh, in_specs=placed, out_specs=P("win", "chan", None), check_vma=False
    )
```

time: 817 us -> 151 us (0.18); the launches traced: 808 us -> 150 us
  other arithmetic: 327 us -> 2.72 us
  waiting for transfers between devices: 172 us -> 0 us
  local copies, waits for them, and re-layouts: 167 us -> 8.73 us
  Pallas kernels: 0 us -> 139 us
  matrix products: 82.2 us -> 0 us
  starting transfers between devices: 40.6 us -> 0 us
  between operations: 14 us -> 0.04 us
    dot_general x8 -> x0, other arithmetic: 286 us -> none  [one_offset(): jnp.einsum('wcf,wcf->cf', whitened[1], partner_rows[1], preferred_element...]
    pallas_call x0 -> x2, Pallas kernels: none -> 139 us  [the longest x1 137 us: on_device(): pl.pallas_call(stack_kernel, out_shape=jax.ShapeDtypeStruct((channels, sh...]
    gather x8 -> x0, local copies, waits for them, and re-layouts: 121 us -> none  [one_offset(): lax.dynamic_slice_in_dim(extended, shift_by + reach_span, channels, 2)]
    ppermute x16 -> x0, waiting for transfers between devices: 88.3 us -> none  [passed_along(): lax.ppermute(value, axis, [(source, source + steps) for source in range(f...]
    reduce_scatter x1 -> x0, waiting for transfers between devices: 84.1 us -> none  [on_device(): lax.psum_scatter(jnp.einsum('cjo,oct->jct', picker, by_offset, precision=...]
    dot_general x9 -> x0, matrix products: 82.2 us -> none  [the longest x8 69.9 us: offset_block(): jnp.dot(joined, basis, precision=lax.Precision.HIGHEST, preferred_element...]
    ppermute x16 -> x0, starting transfers between devices: 40.6 us -> none  [passed_along(): lax.ppermute(value, axis, [(source, source + steps) for source in range(f...]
    while x49 -> x0, local copies, waits for them, and re-layouts: 35.1 us -> none  [the longest x1 30.1 us: on_device(): lax.map(offset_block, jnp.arange(slots // group, dtype=jnp.int32))]
  transfers between devices with their start and end apart: 17 -> 0, of which waited for: 8 -> 0; matrix products, arithmetic and copies ran while one was open for 1% -> 0% of each run, Pallas kernels for 0% -> 0%
where the time goes in v1:
time: 151 us; the launch traced here: 150 us
  Pallas kernels  139 us (92%)
  local copies, waits for them, and re-layouts  8.73 us (6%)
  other arithmetic  2.72 us (2%)
    pallas_call x1, Pallas kernels, on_device(): pl.pallas_call(stack_kernel, out_shape=jax.ShapeDtypeStruct((channels, sh...  137 us
    unnamed x10, local copies, waits for them, and re-layouts  5.07 us

profile of v1, /device:TPU:1, one launch (start us, length us, event | category | flops | bytes accessed | tf_op | source)
XLA Modules:
  0.0 150.2 jit_solution(2954676120141439300)
XLA Ops:
  0.0 0.7 fusion
  0.7 0.1 copy.11.live_ref
  0.7 0.7 select_bitcast_fusion
  1.5 0.0 copy-start
  1.5 1.6 %copy-done = bf16[1024,1024]{1,0:T(8,128)(2,1)S(1)} copy-done((bf16[1024,1024]{1,0:T(8,128)(2,1)S(1)}, bf16[1024,1024]{1,0:T(8,128)(2,1)}, u32[]{:S(2)}) %copy-start) | copy-done | bytes 2097176
  3.1 0.0 copy-start.1
  3.1 1.0 copy-done.1
  4.1 0.0 copy-start.4
  4.1 0.9 copy-done.4
  5.0 1.9 %whiten.1 = (bf16[6,16,2560]{2,1,0:T(8,128)(2,1)S(1)}, bf16[6,16,2560]{2,1,0:T(8,128)(2,1)S(1)}) custom-call(bf16[2,5,16,1536]{3,2,1,0:T(8,128)(2,1)S(1)} %copy-done.1, f32[16,1]{1,0:T(8,128)S(1)} %copy.11.live_ref, bf16[1024,1024]{1,0:T(8,128)(2,1)S(1)} %copy-done, bf16[256,256]{1,0:T(8,128)(2,1)S(1)} %copy-done.4), custom_call_target="tpu_custom_call" | custom-call | tf_op jit(solution)/shard_map/whiten/pallas_call | solution.py:297
  6.9 0.0 copy-start.2
  7.0 0.8 copy-done.2
  7.7 0.0 copy-start.3
  7.7 0.8 copy-done.3
  8.5 2.0 %copy.12.rel_ref = s32[16,256,1]{2,1,0:T(8,128)} copy(s32[16,256,1]{1,0,2:T(8,128)S(1)} %select_bitcast_fusion) | data formatting | bytes 32768 | tf_op jit(solution)/shard_map/broadcast_in_dim | solution.py:308
  10.5 136.8 %stack.1 = f32[16,64,256]{2,1,0:T(8,128)} custom-call(bf16[6,16,2560]{2,1,0:T(8,128)(2,1)} %copy-done.2, bf16[6,16,2560]{2,1,0:T(8,128)(2,1)} %copy-done.3, bf16[6,256,256]{2,1,0:T(8,128)(2,1)} %constant.25.clone.cos_ref, bf16[6,256,256]{2,1,0:T(8,128)(2,1)} %constant.26.clone.sin_ref, s32[16,256,1]{2,1,0:T(8,128)} %copy.12.rel_ref), custom_call_target="tpu_custom_call" | custom-call | tf_op jit(solution)/shard_map/stack/pallas_call | solution.py:309
  147.3 1.3 multiply_bitcast_fusion
  148.6 1.6 %copy.13 = f32[64,16,256]{2,1,0:T(8,128)} copy(f32[64,16,256]{2,0,1:T(8,128)S(1)} %multiply_bitcast_fusion) | data formatting | bytes 2097152 | tf_op jit(solution)/shard_map/mul | solution.py:341
Async XLA Ops:
  1.5 1.6 %copy-start = (bf16[1024,1024]{1,0:T(8,128)(2,1)S(1)}, bf16[1024,1024]{1,0:T(8,128)(2,1)}, u32[]{:S(2)}) copy-start(bf16[1024,1024]{1,0:T(8,128)(2,1)} %constant.23.clone.main_ref) | copy-start | bytes 6291460
  3.1 1.0 copy-start.1
  4.1 0.9 copy-start.4
  6.9 0.8 copy-start.2
  7.7 0.8 copy-start.3

commit v2 on v1

--- a/solution.py
+++ b/solution.py
@@ -15,7 +15,8 @@
 water_level = 0.1
 
 MESH = pl.DeviceIdType.MESH
-BLOCKS = 7
+OFFSETS = (1, -2, 3, -4, 5, -6, 7)
+BLOCKS = len(OFFSETS)
 TILE = 128
 SUB = 16
 QUAD = 64
@@ -104,33 +105,30 @@
     other_core = win + 1 - 2 * core
     other_far = lax.rem(win + 2, 4)
 
-    def above(distance):
-        return lax.rem(me + distance, count)
-
-    def below(distance):
-        return lax.rem(me + count - distance, count)
+    def block(offset):
+        return lax.rem(me + count + offset, count)
 
     barrier = pltpu.get_barrier_semaphore()
-    for distance in range(1, BLOCKS + 1):
-        for chan in (above(distance), below(distance)):
+    for offset in OFFSETS:
+        for chan in (block(offset), block(-offset)):
             pl.semaphore_signal(barrier, inc=1, device_id={"chan": chan, "win": win}, device_id_type=MESH)
     for partner in (other_core, other_far):
         pl.semaphore_signal(barrier, inc=1, device_id={"chan": me, "win": partner}, device_id_type=MESH)
     pl.semaphore_wait(barrier, 2 * BLOCKS + 2)
 
-    def halo(chunk, distance):
+    def halo(chunk, place):
         return pltpu.make_async_remote_copy(
             src_ref=x_ref.at[chunk],
-            dst_ref=around.at[chunk, pl.ds(distance * channels, channels), :],
-            send_sem=halo_send.at[chunk, distance - 1],
-            recv_sem=halo_recv.at[chunk, distance - 1],
-            device_id={"chan": below(distance), "win": win},
+            dst_ref=around.at[chunk, pl.ds((place + 1) * channels, channels), :],
+            send_sem=halo_send.at[chunk, place],
+            recv_sem=halo_recv.at[chunk, place],
+            device_id={"chan": block(-OFFSETS[place]), "win": win},
             device_id_type=MESH,
         )
 
     for chunk in range(chunks):
-        for distance in range(1, BLOCKS + 1):
-            halo(chunk, distance).start()
+        for place in range(BLOCKS):
+            halo(chunk, place).start()
     for chunk in range(chunks):
         around[chunk, :channels, :] = x_ref[chunk]
     even[...] = jnp.zeros_like(even)
@@ -145,8 +143,8 @@
         masks.append(jnp.concatenate([main, rest], axis=1).astype(jnp.bfloat16))
 
     def one_chunk(chunk, _):
-        for distance in range(1, BLOCKS + 1):
-            halo(chunk, distance).wait_recv()
+        for place in range(BLOCKS):
+            halo(chunk, place).wait_recv()
 
         def one_quad(quad, _):
             start = pl.multiple_of(quad * QUAD_LANES, TILE)
@@ -187,39 +185,44 @@
         sin_sum = odd[channel]
         ahead[channel] = (cos_sum - sin_sum).astype(jnp.bfloat16)
         mirrored = (cos_sum + sin_sum).astype(jnp.bfloat16)
-        for distance in range(1, BLOCKS + 1):
-            back_out[distance - 1, channel] = mirrored[distance * channels : (distance + 1) * channels]
+        for place in range(BLOCKS):
+            back_out[place, channel] = mirrored[(place + 1) * channels : (place + 2) * channels]
         return 0
 
     lax.fori_loop(0, channels, lags_of, 0)
 
-    def back(distance):
+    def back(place):
         return pltpu.make_async_remote_copy(
-            src_ref=back_out.at[distance - 1],
-            dst_ref=back_in.at[distance - 1],
-            send_sem=back_send.at[distance - 1],
-            recv_sem=back_recv.at[distance - 1],
-            device_id={"chan": above(distance), "win": win},
+            src_ref=back_out.at[place],
+            dst_ref=back_in.at[place],
+            send_sem=back_send.at[place],
+            recv_sem=back_recv.at[place],
+            device_id={"chan": block(OFFSETS[place]), "win": win},
             device_id_type=MESH,
         )
 
-    for distance in range(1, BLOCKS + 1):
-        back(distance).start()
-    for distance in range(1, BLOCKS + 1):
-        back(distance).wait_recv()
+    for place in range(BLOCKS):
+        back(place).start()
+    for place in range(BLOCKS):
+        back(place).wait_recv()
 
     slots = rel_ref.shape[1]
+
+    lane = lax.broadcasted_iota(jnp.int32, (1, span), 1)
+    held = lane
+    for place, offset in enumerate(OFFSETS):
+        held = jnp.where(lane // channels == place + 1, lane + (offset - place - 1) * channels, held)
 
     def pick(channel, _):
         target = rel_ref[channel]
-        lanes = lax.broadcasted_iota(jnp.int32, (slots, span), 1)
+        lanes = jnp.broadcast_to(held, (slots, span))
         chosen = (lanes == target).astype(jnp.float32).astype(jnp.bfloat16)
         total = jnp.dot(chosen, ahead[channel], preferred_element_type=jnp.float32)
         lanes = lax.broadcasted_iota(jnp.int32, (slots, channels * channels), 1)
-        for distance in range(1, BLOCKS + 1):
-            place = (target + distance * channels) * channels + channel
-            chosen = (lanes == place).astype(jnp.float32).astype(jnp.bfloat16)
-            rows = back_in[distance - 1].reshape(channels * channels, LAGS)
+        for place in range(BLOCKS):
+            wanted = (target + OFFSETS[place] * channels) * channels + channel
+            chosen = (lanes == wanted).astype(jnp.float32).astype(jnp.bfloat16)
+            rows = back_in[place].reshape(channels * channels, LAGS)
             total += jnp.dot(chosen, rows, preferred_element_type=jnp.float32)
         picked[channel] = total.astype(jnp.bfloat16)
         return 0
@@ -273,10 +276,10 @@
     lax.fori_loop(0, channels, last_sum, 0)
 
     for chunk in range(chunks):
-        for distance in range(1, BLOCKS + 1):
-            halo(chunk, distance).wait_send()
-    for distance in range(1, BLOCKS + 1):
-        back(distance).wait_send()
+        for place in range(BLOCKS):
+            halo(chunk, place).wait_send()
+    for place in range(BLOCKS):
+        back(place).wait_send()
     for half in range(2):
         to_core(half).wait_send()
     away.wait_send()

time: 151 us -> 117 us (0.77)
  Pallas kernels: 139 us -> 105 us
    pallas_call x1, Pallas kernels: 137 us -> 103 us  [on_device(): pl.pallas_call(stack_kernel, out_shape=jax.ShapeDtypeStruct((channels, sh...]
where the time goes in v2:
time: 117 us
  Pallas kernels  105 us (90%)
  local copies, waits for them, and re-layouts  8.73 us (7%)
  other arithmetic  2.72 us (2%)
    pallas_call x1, Pallas kernels, on_device(): pl.pallas_call(stack_kernel, out_shape=jax.ShapeDtypeStruct((channels, sh...  103 us
    unnamed x10, local copies, waits for them, and re-layouts  5.07 us

profile of v2, /device:TPU:1, one launch (start us, length us, event | category | flops | bytes accessed | tf_op | source)
XLA Modules:
  0.0 116.6 jit_solution(15752931062915856724)
XLA Ops:
  0.0 0.7 fusion
  0.7 0.1 copy.11.live_ref
  0.7 0.7 select_bitcast_fusion
  1.5 0.0 copy-start
  1.5 1.6 %copy-done = bf16[1024,1024]{1,0:T(8,128)(2,1)S(1)} copy-done((bf16[1024,1024]{1,0:T(8,128)(2,1)S(1)}, bf16[1024,1024]{1,0:T(8,128)(2,1)}, u32[]{:S(2)}) %copy-start) | copy-done | bytes 2097176
  3.1 0.0 copy-start.1
  3.1 1.0 copy-done.1
  4.1 0.0 copy-start.4
  4.1 0.9 copy-done.4
  5.0 1.9 %whiten.1 = (bf16[6,16,2560]{2,1,0:T(8,128)(2,1)S(1)}, bf16[6,16,2560]{2,1,0:T(8,128)(2,1)S(1)}) custom-call(bf16[2,5,16,1536]{3,2,1,0:T(8,128)(2,1)S(1)} %copy-done.1, f32[16,1]{1,0:T(8,128)S(1)} %copy.11.live_ref, bf16[1024,1024]{1,0:T(8,128)(2,1)S(1)} %copy-done, bf16[256,256]{1,0:T(8,128)(2,1)S(1)} %copy-done.4), custom_call_target="tpu_custom_call" | custom-call | tf_op jit(solution)/shard_map/whiten/pallas_call | solution.py:300
  6.9 0.0 copy-start.2
  7.0 0.8 copy-done.2
  7.7 0.0 copy-start.3
  7.7 0.8 copy-done.3
  8.5 2.0 %copy.12.rel_ref = s32[16,256,1]{2,1,0:T(8,128)} copy(s32[16,256,1]{1,0,2:T(8,128)S(1)} %select_bitcast_fusion) | data formatting | bytes 32768 | tf_op jit(solution)/shard_map/broadcast_in_dim | solution.py:311
  10.5 103.2 %stack.1 = f32[16,64,256]{2,1,0:T(8,128)} custom-call(bf16[6,16,2560]{2,1,0:T(8,128)(2,1)} %copy-done.2, bf16[6,16,2560]{2,1,0:T(8,128)(2,1)} %copy-done.3, bf16[6,256,256]{2,1,0:T(8,128)(2,1)} %constant.25.clone.cos_ref, bf16[6,256,256]{2,1,0:T(8,128)(2,1)} %constant.26.clone.sin_ref, s32[16,256,1]{2,1,0:T(8,128)} %copy.12.rel_ref), custom_call_target="tpu_custom_call" | custom-call | tf_op jit(solution)/shard_map/stack/pallas_call | solution.py:312
  113.7 1.3 %multiply_bitcast_fusion = f32[64,16,256]{2,0,1:T(8,128)S(1)} fusion(f32[16,64,256]{2,1,0:T(8,128)} %stack.1), kind=kLoop, calls=%fused_computation | loop fusion | flops 262144 | bytes 2097152 | tf_op jit(solution)/shard_map/mul | solution.py:344
  115.1 1.6 %copy.13 = f32[64,16,256]{2,1,0:T(8,128)} copy(f32[64,16,256]{2,0,1:T(8,128)S(1)} %multiply_bitcast_fusion) | data formatting | bytes 2097152 | tf_op jit(solution)/shard_map/mul | solution.py:344
Async XLA Ops:
  1.5 1.6 %copy-start = (bf16[1024,1024]{1,0:T(8,128)(2,1)S(1)}, bf16[1024,1024]{1,0:T(8,128)(2,1)}, u32[]{:S(2)}) copy-start(bf16[1024,1024]{1,0:T(8,128)(2,1)} %constant.23.clone.main_ref) | copy-start | bytes 6291460
  3.1 1.0 copy-start.1
  4.1 0.9 copy-start.4
  6.9 0.8 copy-start.2
  7.7 0.8 copy-start.3

commit v3 on v2

v3 whole, which is shorter than its diff:
```python
import math

import jax
import jax.numpy as jnp
import numpy as np
from jax import lax
from jax.experimental import pallas as pl
from jax.experimental.pallas import tpu as pltpu
from jax.sharding import PartitionSpec as P

LAGS = 256
SMOOTH = 8
FLO = 64
NSAMP = 6000
water_level = 0.1

MESH = pl.DeviceIdType.MESH
OFFSETS = (1, -2, 3, -4, 5, -6, 7)
BLOCKS = len(OFFSETS)
TILE = 128
SUB = 16
QUAD = 64
QUAD_LANES = 640
CHUNK = 256
CHUNK_LANES = CHUNK // QUAD * QUAD_LANES
GROUPS = 4
ABREAST = 4


def bin_order():
    main = np.zeros((8 * TILE, 8 * TILE), np.float32)
    part, f = np.meshgrid(np.arange(8), np.arange(TILE), indexing="ij")
    main[part * TILE + f, (f // SUB) * TILE + part * SUB + f % SUB] = 1.0
    rest = np.zeros((2 * TILE, 2 * TILE), np.float32)
    part, f = np.meshgrid(np.arange(2), np.arange(TILE), indexing="ij")
    rest[part * TILE + f, (f // QUAD) * TILE + part * QUAD + f % QUAD] = 1.0
    return main.astype(jnp.bfloat16), rest.astype(jnp.bfloat16)


def lag_tables(bins):
    steps = np.mod((FLO + np.arange(bins))[:, None] * (np.arange(LAGS) - LAGS // 2)[None, :], NSAMP)
    angles = steps.astype(np.float64) * (2.0 * math.pi / NSAMP)
    shape = (bins // CHUNK, CHUNK, LAGS)
    return (
        np.cos(angles).astype(np.float32).reshape(shape).astype(jnp.bfloat16),
        np.sin(angles).astype(np.float32).reshape(shape).astype(jnp.bfloat16),
    )


def kernel(
    spectra_ref, partners_ref, mask_ref, gap_ref, main_ref, rest_ref, cos_ref, sin_ref, out_ref,
    spectra, partners, mask, main, rest, cos_table, sin_table,
    held, turned, around, cross, even, odd, chosen, mirrored, lags, back_out, picked, from_core, to_far, from_far,
    load_sem, halo_send, halo_recv, back_send, back_recv, core_send, core_recv, far_send, far_recv,
):
    windows, channels, bins = spectra.shape[1:]
    tiles = bins // TILE
    chunks = bins // CHUNK
    span = around.shape[1]
    slots = partners.shape[1]
    share = slots // 4
    few = channels // GROUPS
    count = lax.axis_size("chan")
    me = lax.axis_index("chan")
    win = lax.axis_index("win")
    core = lax.rem(win, 2)
    far = win // 2
    other_core = win + 1 - 2 * core
    other_far = lax.rem(win + 2, 4)

    def block(offset):
        return lax.rem(me + count + offset, count)

    loads = [(spectra_ref.at[:, window], spectra.at[:, window]) for window in range(windows)]
    loads += [(main_ref, main), (rest_ref, rest), (partners_ref, partners), (mask_ref, mask)]
    loads += [(cos_ref, cos_table), (sin_ref, sin_table)]
    loads = [pltpu.make_async_copy(source, target, load_sem.at[i]) for i, (source, target) in enumerate(loads)]
    for load in loads:
        load.start()
    barrier = pltpu.get_barrier_semaphore()
    for offset in OFFSETS:
        for chan in (block(offset), block(-offset)):
            pl.semaphore_signal(barrier, inc=1, device_id={"chan": chan, "win": win}, device_id_type=MESH)
    for partner in (other_core, other_far):
        pl.semaphore_signal(barrier, inc=1, device_id={"chan": me, "win": partner}, device_id_type=MESH)

    position = lax.broadcasted_iota(jnp.int32, (1, bins), 1)
    bin_count = jnp.minimum(position + SMOOTH, bins - 1) - jnp.maximum(position - SMOOTH, 0) + 1
    inverse = 1.0 / bin_count.astype(jnp.float32)
    row = lax.broadcasted_iota(jnp.int32, (channels, 1), 0)
    live = jnp.zeros((channels, 1), jnp.float32)
    for channel in range(channels):
        live = jnp.where(row == channel, jnp.where(gap_ref[channel] == 0, 1.0, 0.0), live)
    pad = jnp.zeros((channels, TILE), jnp.float32)
    for window in range(windows):
        loads[window].wait()
        real_part = spectra[0, window].astype(jnp.float32)
        imag_part = spectra[1, window].astype(jnp.float32)
        magnitude = jnp.sqrt(real_part * real_part + imag_part * imag_part)
        band_mean = jnp.sum(magnitude, axis=1, keepdims=True) * (1.0 / bins)
        padded = jnp.concatenate([magnitude, pad], axis=1)
        width = bins + TILE
        total = padded
        for step in (1, 2, 4, 8):
            total = total + pltpu.roll(total, step, 1)
        near = pltpu.roll(total, width - SMOOTH, 1) + pltpu.roll(padded, SMOOTH, 1)
        divisor = near[:, :bins] * inverse + water_level * band_mean + 1e-06
        factor = live / divisor
        white_real = (real_part * factor).astype(jnp.bfloat16)
        white_imag = (imag_part * factor).astype(jnp.bfloat16)
        for tile in range(tiles):
            rows = slice(tile * channels, (tile + 1) * channels)
            lanes = slice(tile * TILE, (tile + 1) * TILE)
            held[rows, 2 * window * TILE : (2 * window + 1) * TILE] = white_real[:, lanes]
            held[rows, (2 * window + 1) * TILE : (2 * window + 2) * TILE] = white_imag[:, lanes]

    def ordered(source, store):
        first = jnp.dot(source[:, : 8 * TILE], main[...], preferred_element_type=jnp.float32).astype(jnp.bfloat16)
        last = jnp.dot(source[:, 8 * TILE :], rest[...], preferred_element_type=jnp.float32).astype(jnp.bfloat16)
        for tile in range(tiles):
            rows = slice(tile * channels, (tile + 1) * channels)
            for half in range(2):
                quad = tile * 2 + half
                chunk, start = quad // (CHUNK // QUAD), quad % (CHUNK // QUAD) * QUAD_LANES
                store(chunk, slice(start, start + 4 * TILE), first[rows, half * 4 * TILE : (half + 1) * 4 * TILE])
                store(
                    chunk, slice(start + 4 * TILE, start + QUAD_LANES), last[rows, half * TILE : (half + 1) * TILE]
                )

    def store_around(chunk, lanes, value):
        around[chunk, :channels, lanes] = value

    def store_turned(chunk, lanes, value):
        turned[chunk, :, lanes] = value

    loads[windows].wait()
    loads[windows + 1].wait()
    ordered(held[...], store_around)

    def halo(chunk, place):
        return pltpu.make_async_remote_copy(
            src_ref=around.at[chunk, pl.ds(0, channels), :],
            dst_ref=around.at[chunk, pl.ds((place + 1) * channels, channels), :],
            send_sem=halo_send.at[chunk, place],
            recv_sem=halo_recv.at[chunk, place],
            device_id={"chan": block(-OFFSETS[place]), "win": win},
            device_id_type=MESH,
        )

    pl.semaphore_wait(barrier, 2 * BLOCKS + 2)
    for chunk in range(chunks):
        for place in range(BLOCKS):
            halo(chunk, place).start()

    parts = held[...]
    swapped = [parts[:, (i ^ 1) * TILE : ((i ^ 1) + 1) * TILE] for i in range(2 * windows)]
    swapped = [-one if i % 2 else one for i, one in enumerate(swapped)]
    ordered(jnp.concatenate(swapped, axis=1), store_turned)
    even[...] = jnp.zeros_like(even)
    odd[...] = jnp.zeros_like(odd)
    lags[:, span + BLOCKS * channels :, :] = jnp.zeros((channels, channels, LAGS), jnp.bfloat16)

    loads[windows + 2].wait()
    loads[windows + 3].wait()
    lane = lax.broadcasted_iota(jnp.int32, (1, 2 * span), 1)
    column = lane
    for place, offset in enumerate(OFFSETS):
        column = jnp.where(lane // channels == place + 1, lane + (offset - place - 1) * channels, column)
        column = jnp.where(lane // channels == place + 1 + BLOCKS, lane - (offset + place + 1 + BLOCKS) * channels, column)
    column = jnp.where(lane // channels == 2 * BLOCKS + 1, 2**20, column).astype(jnp.float32)
    relative = jnp.where(mask[...] > 0, partners[...] - me * channels, -(2**20)).astype(jnp.float32)
    relative = jnp.concatenate([relative, jnp.zeros((TILE - channels, slots), jnp.float32)], axis=0).T
    for channel in range(channels):
        match = relative[:, channel : channel + 1] == column
        chosen[channel] = jnp.where(match, 1.0, 0.0).astype(jnp.bfloat16)

    row = lax.broadcasted_iota(jnp.int32, (SUB, TILE), 0)
    lane = lax.broadcasted_iota(jnp.int32, (SUB, TILE), 1)
    masks = []
    for group in range(QUAD // SUB):
        first = (lane % SUB == row).astype(jnp.float32)
        last = (lane % QUAD == group * SUB + row).astype(jnp.float32)
        masks.append(jnp.concatenate([first, last], axis=1).astype(jnp.bfloat16))
    loads[windows + 4].wait()
    loads[windows + 5].wait()

    def one_chunk(chunk, _):
        for place in range(BLOCKS):
            halo(chunk, place).wait_recv()

        def one_quad(quad, _):
            start = pl.multiple_of(quad * QUAD_LANES, TILE)

            def lane_tiles(ref, rows, group):
                first = ref[chunk, :rows, pl.ds(pl.multiple_of(start + group * TILE, TILE), TILE)]
                last = ref[chunk, :rows, pl.ds(pl.multiple_of(start + 4 * TILE, TILE), TILE)]
                return jnp.concatenate([first, last], axis=1)

            for group in range(QUAD // SUB):
                others = lane_tiles(around, span, group)
                for part, ref in ((0, around), (1, turned)):
                    own = lane_tiles(ref, channels, group)
                    spread = (own[:, None, :] * masks[group][None, :, :]).reshape(channels * SUB, 2 * TILE)
                    product = lax.dot_general(
                        spread, others, (((1,), (1,)), ((), ())), preferred_element_type=jnp.float32
                    )
                    first_bin = pl.multiple_of(quad * QUAD + group * SUB, SUB)
                    cross[part, :, pl.ds(first_bin, SUB), :] = product.astype(jnp.bfloat16).reshape(channels, SUB, span)
            return 0

        lax.fori_loop(0, CHUNK // QUAD, one_quad, 0)

        def some_channels(number, _):
            first = number * ABREAST
            for part, table, total in ((0, cos_table, even), (1, sin_table, odd)):
                rows = jnp.concatenate([cross[part, first + i].T for i in range(ABREAST)], axis=0)
                result = jnp.dot(rows, table[chunk], preferred_element_type=jnp.float32)
                total[pl.ds(first, ABREAST)] += result.reshape(ABREAST, span, LAGS)
            return 0

        lax.fori_loop(0, channels // ABREAST, some_channels, 0)
        return 0

    lax.fori_loop(0, chunks, one_chunk, 0)

    for channel in range(channels):
        cos_sum = even[channel]
        sin_sum = odd[channel]
        lags[channel, :span, :] = (cos_sum - sin_sum).astype(jnp.bfloat16)
        back_sum = (cos_sum + sin_sum)[channels:]
        for half in range(LAGS // TILE):
            lanes = slice(half * TILE, (half + 1) * TILE)
            mirrored[half, pl.ds(channel, BLOCKS * channels, stride=channels), :] = back_sum[:, lanes]

    def back(group, place):
        return pltpu.make_async_remote_copy(
            src_ref=back_out.at[group, place],
            dst_ref=lags.at[pl.ds(group * few, few), pl.ds(span + place * channels, channels), :],
            send_sem=back_send.at[group, place],
            recv_sem=back_recv.at[group, place],
            device_id={"chan": block(OFFSETS[place]), "win": win},
            device_id_type=MESH,
        )

    for group in range(GROUPS):
        for place in range(BLOCKS):
            first = (place * channels + group * few) * channels
            for half in range(LAGS // TILE):
                rows = mirrored[half, first : first + few * channels].astype(jnp.bfloat16)
                lanes = slice(half * TILE, (half + 1) * TILE)
                back_out[group, place, :, :, lanes] = rows.reshape(few, channels, TILE)
            back(group, place).start()

    def slots_of(owner):
        return pl.ds(pl.multiple_of(owner * share, share), share)

    def to_core(group, half):
        return pltpu.make_async_remote_copy(
            src_ref=picked.at[pl.ds(group * few, few), slots_of(2 * half + 1 - core), :],
            dst_ref=from_core.at[half, pl.ds(group * few, few)],
            send_sem=core_send.at[group, half],
            recv_sem=core_recv.at[group, half],
            device_id={"chan": me, "win": other_core},
            device_id_type=MESH,
        )

    def away(group):
        return pltpu.make_async_remote_copy(
            src_ref=to_far.at[pl.ds(group * few, few)],
            dst_ref=from_far.at[pl.ds(group * few, few)],
            send_sem=far_send.at[group],
            recv_sem=far_recv.at[group],
            device_id={"chan": me, "win": other_far},
            device_id_type=MESH,
        )

    for group in range(GROUPS + 1):
        if group < GROUPS:
            for place in range(BLOCKS):
                back(group, place).wait_recv()
            for channel in range(group * few, (group + 1) * few):
                rows = jnp.dot(chosen[channel], lags[channel], preferred_element_type=jnp.float32)
                picked[channel] = rows.astype(jnp.bfloat16)
            for half in range(2):
                to_core(group, half).start()
        if group > 0:
            for half in range(2):
                to_core(group - 1, half).wait_recv()
            for channel in range((group - 1) * few, group * few):
                mine = picked[channel, slots_of(other_far), :].astype(jnp.float32)
                theirs = from_core[1 - far, channel].astype(jnp.float32)
                to_far[channel] = (mine + theirs).astype(jnp.bfloat16)
            away(group - 1).start()
    scale = 1.0 / math.sqrt(windows * lax.axis_size("win") * bins)
    for group in range(GROUPS):
        away(group).wait_recv()
        for channel in range(group * few, (group + 1) * few):
            mine = picked[channel, slots_of(win), :].astype(jnp.float32)
            theirs = from_core[far, channel].astype(jnp.float32) + from_far[channel].astype(jnp.float32)
            for half in range(LAGS // TILE):
                lanes = slice(half * TILE, (half + 1) * TILE)
                out_ref[half, pl.ds(channel, share, stride=channels), :] = ((mine + theirs) * scale)[:, lanes]

    for chunk in range(chunks):
        for place in range(BLOCKS):
            halo(chunk, place).wait_send()
    for group in range(GROUPS):
        for place in range(BLOCKS):
            back(group, place).wait_send()
        for half in range(2):
            to_core(group, half).wait_send()
        away(group).wait_send()


def on_device(spectra, partners, pair_mask, gap_flags):
    _, windows, channels, bins = spectra.shape
    slots = partners.shape[1]
    chunks = bins // CHUNK
    span = (BLOCKS + 1) * channels
    share = slots // 4
    bf16 = jnp.bfloat16
    main, rest = bin_order()
    cos_table, sin_table = lag_tables(bins)
    anywhere = pl.BlockSpec(memory_space=pl.ANY)
    scalars = pl.BlockSpec(memory_space=pltpu.SMEM)
    semaphores = pltpu.SemaphoreType.DMA
    stacked = pl.pallas_call(
        kernel,
        out_shape=jax.ShapeDtypeStruct((LAGS // TILE, share * channels, TILE), jnp.float32),
        in_specs=[anywhere] * 3 + [scalars] + [anywhere] * 4,
        out_specs=pl.BlockSpec(memory_space=pltpu.VMEM),
        scratch_shapes=[
            pltpu.VMEM(spectra.shape, bf16),
            pltpu.VMEM(partners.shape, jnp.int32),
            pltpu.VMEM(pair_mask.shape, jnp.int32),
            pltpu.VMEM(main.shape, bf16),
            pltpu.VMEM(rest.shape, bf16),
            pltpu.VMEM(cos_table.shape, bf16),
            pltpu.VMEM(sin_table.shape, bf16),
            pltpu.VMEM((bins // TILE * channels, 2 * windows * TILE), bf16),
            pltpu.VMEM((chunks, channels, CHUNK_LANES), bf16),
            pltpu.VMEM((chunks, span, CHUNK_LANES), bf16),
            pltpu.VMEM((2, channels, CHUNK, span), bf16),
            pltpu.VMEM((channels, span, LAGS), jnp.float32),
            pltpu.VMEM((channels, span, LAGS), jnp.float32),
            pltpu.VMEM((channels, slots, 2 * span), bf16),
            pltpu.VMEM((LAGS // TILE, BLOCKS * channels * channels, TILE), jnp.float32),
            pltpu.VMEM((channels, 2 * span, LAGS), bf16),
            pltpu.VMEM((GROUPS, BLOCKS, channels // GROUPS, channels, LAGS), bf16),
            pltpu.VMEM((channels, slots, LAGS), bf16),
            pltpu.VMEM((2, channels, share, LAGS), bf16),
            pltpu.VMEM((channels, share, LAGS), bf16),
            pltpu.VMEM((channels, share, LAGS), bf16),
            semaphores((windows + 6,)),
            semaphores((chunks, BLOCKS)),
            semaphores((chunks, BLOCKS)),
            semaphores((GROUPS, BLOCKS)),
            semaphores((GROUPS, BLOCKS)),
            semaphores((GROUPS, 2)),
            semaphores((GROUPS, 2)),
            semaphores((GROUPS,)),
            semaphores((GROUPS,)),
        ],
        compiler_params=pltpu.CompilerParams(
            collective_id=0, has_side_effects=True, vmem_limit_bytes=56 * 2**20
        ),
        name="stack",
    )(spectra, partners, pair_mask, gap_flags, main, rest, cos_table, sin_table)
    stacked = stacked.reshape(LAGS // TILE, share, channels, TILE)
    return jnp.transpose(stacked, (1, 2, 0, 3)).reshape(share, channels, LAGS)


def solution(mesh):
    placed = (P(None, "win", "chan", None), P("chan", None), P("chan", None), P("chan"))
    return jax.shard_map(
        on_device, mesh=mesh, in_specs=placed, out_specs=P("win", "chan", None), check_vma=False
    )
```

time: 117 us -> 91.4 us (0.78)
  Pallas kernels: 105 us -> 88.9 us
  local copies, waits for them, and re-layouts: 8.73 us -> 2.34 us
  other arithmetic: 2.72 us -> 0 us
    pallas_call x2 -> x1, Pallas kernels: 105 us -> 88.9 us  [on_device(): pl.pallas_call(kernel, out_shape=jax.ShapeDtypeStruct((LAGS // TILE, shar...]
    unnamed x10 -> x0, local copies, waits for them, and re-layouts: 5.07 us -> none
    reshape x0 -> x1, local copies, waits for them, and re-layouts: none -> 2.34 us  [on_device(): return jnp.transpose(stacked, (1, 2, 0, 3)).reshape(share, channels, LAGS)]
    broadcast_in_dim x2 -> x0, local copies, waits for them, and re-layouts: 2.07 us -> none  [the longest x1 1.99 us: on_device(): rel = jnp.where(pair_mask > 0, partners - first, -2 ** 20)[:, :, None]]
    mul x1 -> x0, local copies, waits for them, and re-layouts: 1.58 us -> none  [on_device(): return jnp.transpose(stacked, (1, 0, 2)) * scale]
    broadcast_in_dim x2 -> x0, other arithmetic: 1.4 us -> none  [the longest x1 0.74 us: on_device(): rel = jnp.where(pair_mask > 0, partners - first, -2 ** 20)[:, :, None]]
    mul x1 -> x0, other arithmetic: 1.33 us -> none  [on_device(): return jnp.transpose(stacked, (1, 0, 2)) * scale]
where the time goes in v3:
time: 91.4 us; the launch traced here: 91.2 us
  Pallas kernels  88.9 us (97%)
  local copies, waits for them, and re-layouts  2.34 us (3%)
    pallas_call x1, Pallas kernels, on_device(): pl.pallas_call(kernel, out_shape=jax.ShapeDtypeStruct((LAGS // TILE, shar...  88.9 us
    reshape x1, local copies, waits for them, and re-layouts, on_device(): return jnp.transpose(stacked, (1, 2, 0, 3)).reshape(share, channels, LAGS)  2.34 us

profile of v3, /device:TPU:1, one launch (start us, length us, event | category | flops | bytes accessed | tf_op | source)
XLA Modules:
  0.0 91.2 jit_solution(6931587124577572702)
XLA Ops:
  0.0 88.9 %stack.1 = f32[2,1024,128]{2,1,0:T(8,128)} custom-call(bf16[2,5,16,1536]{3,2,1,0:T(8,128)(2,1)} %spectra_ref.1, s32[16,256]{1,0:T(8,128)} %partners_ref.1, s32[16,256]{1,0:T(8,128)} %mask_ref.1, s32[16]{0:T(128)} %gap_ref.1, bf16[1024,1024]{1,0:T(8,128)(2,1)} %constant.8.clone.main_ref, bf16[256,256]{1,0:T(8,128)(2,1)} %constant.9.clone.rest_ref, ...), custom_call_target="tpu_custom_call" | custom-call | tf_op jit(solution)/shard_map/stack/pallas_call | solution.py:327
  88.9 2.3 %copy.12 = f32[2,64,2,8,128]{4,3,0,2,1:T(8,128)} copy(f32[2,64,2,8,128]{4,3,2,1,0:T(8,128)} %bitcast.7) | data formatting | bytes 2097152 | tf_op jit(solution)/shard_map/reshape | solution.py:370

commit v4 on v3

--- a/solution.py
+++ b/solution.py
@@ -15,15 +15,19 @@
 water_level = 0.1
 
 MESH = pl.DeviceIdType.MESH
-OFFSETS = (1, -2, 3, -4, 5, -6, 7)
+OFFSETS = (1, -2, 3, 4, -5, -6, 7)
 BLOCKS = len(OFFSETS)
+FIRST, SECOND = 1, 5
+RELAY = OFFSETS[SECOND] - OFFSETS[FIRST]
+LAST = BLOCKS - 1
+EDGE = 4
 TILE = 128
 SUB = 16
 QUAD = 64
 QUAD_LANES = 640
 CHUNK = 256
 CHUNK_LANES = CHUNK // QUAD * QUAD_LANES
-GROUPS = 4
+GROUPS = 8
 ABREAST = 4
 
 
@@ -50,7 +54,7 @@
 def kernel(
     spectra_ref, partners_ref, mask_ref, gap_ref, main_ref, rest_ref, cos_ref, sin_ref, out_ref,
     spectra, partners, mask, main, rest, cos_table, sin_table,
-    held, turned, around, cross, even, odd, chosen, mirrored, lags, back_out, picked, from_core, to_far, from_far,
+    held, turned, around, edge_out, edge_in, cross, even, odd, chosen, mirrored, lags, back_out, picked, from_core, to_far, from_far,
     load_sem, halo_send, halo_recv, back_send, back_recv, core_send, core_recv, far_send, far_recv,
 ):
     windows, channels, bins = spectra.shape[1:]
@@ -115,8 +119,9 @@
             held[rows, (2 * window + 1) * TILE : (2 * window + 2) * TILE] = white_imag[:, lanes]
 
     def ordered(source, store):
-        first = jnp.dot(source[:, : 8 * TILE], main[...], preferred_element_type=jnp.float32).astype(jnp.bfloat16)
-        last = jnp.dot(source[:, 8 * TILE :], rest[...], preferred_element_type=jnp.float32).astype(jnp.bfloat16)
+        wide_first = jnp.dot(source[:, : 8 * TILE], main[...], preferred_element_type=jnp.float32)
+        wide_last = jnp.dot(source[:, 8 * TILE :], rest[...], preferred_element_type=jnp.float32)
+        first, last = wide_first.astype(jnp.bfloat16), wide_last.astype(jnp.bfloat16)
         for tile in range(tiles):
             rows = slice(tile * channels, (tile + 1) * channels)
             for half in range(2):
@@ -126,6 +131,7 @@
                 store(
                     chunk, slice(start + 4 * TILE, start + QUAD_LANES), last[rows, half * TILE : (half + 1) * TILE]
                 )
+        return wide_first, wide_last
 
     def store_around(chunk, lanes, value):
         around[chunk, :channels, lanes] = value
@@ -135,22 +141,42 @@
 
     loads[windows].wait()
     loads[windows + 1].wait()
-    ordered(held[...], store_around)
+    wide_first, wide_last = ordered(held[...], store_around)
+    for chunk in range(chunks):
+        pieces = []
+        for quad in range(CHUNK // QUAD):
+            tile, half = divmod(chunk * (CHUNK // QUAD) + quad, 2)
+            rows = slice(tile * channels, tile * channels + EDGE)
+            first = wide_first[rows, half * 4 * TILE : (half + 1) * 4 * TILE]
+            last = wide_last[rows, half * TILE : (half + 1) * TILE]
+            pieces.append(jnp.concatenate([first, last], axis=1))
+        edge_out[chunk] = jnp.concatenate(pieces, axis=0).astype(jnp.bfloat16)
 
     def halo(chunk, place):
+        if place == LAST:
+            source, target = edge_out.at[chunk], edge_in.at[chunk]
+        else:
+            first = (FIRST + 1) * channels if place == SECOND else 0
+            source = around.at[chunk, pl.ds(first, channels), :]
+            target = around.at[chunk, pl.ds((place + 1) * channels, channels), :]
         return pltpu.make_async_remote_copy(
-            src_ref=around.at[chunk, pl.ds(0, channels), :],
-            dst_ref=around.at[chunk, pl.ds((place + 1) * channels, channels), :],
+            src_ref=source,
+            dst_ref=target,
             send_sem=halo_send.at[chunk, place],
             recv_sem=halo_recv.at[chunk, place],
-            device_id={"chan": block(-OFFSETS[place]), "win": win},
+            device_id={"chan": block(-RELAY if place == SECOND else -OFFSETS[place]), "win": win},
             device_id_type=MESH,
         )
 
     pl.semaphore_wait(barrier, 2 * BLOCKS + 2)
+    halo(0, FIRST).start()
+    halo(1, FIRST).start()
     for chunk in range(chunks):
         for place in range(BLOCKS):
-            halo(chunk, place).start()
+            if place not in (FIRST, SECOND):
+                halo(chunk, place).start()
+        if chunk + 2 < chunks:
+            halo(chunk + 2, FIRST).start()
 
     parts = held[...]
     swapped = [parts[:, (i ^ 1) * TILE : ((i ^ 1) + 1) * TILE] for i in range(2 * windows)]
@@ -159,6 +185,9 @@
     even[...] = jnp.zeros_like(even)
     odd[...] = jnp.zeros_like(odd)
     lags[:, span + BLOCKS * channels :, :] = jnp.zeros((channels, channels, LAGS), jnp.bfloat16)
+    lags[EDGE:, span + LAST * channels : span + BLOCKS * channels, :] = jnp.zeros(
+        (channels - EDGE, channels, LAGS), jnp.bfloat16
+    )
 
     loads[windows + 2].wait()
     loads[windows + 3].wait()
@@ -184,9 +213,25 @@
     loads[windows + 4].wait()
     loads[windows + 5].wait()
 
+    def relay(chunk):
+        halo(chunk, FIRST).wait_recv()
+        halo(chunk, SECOND).start()
+
+    relay(0)
+
     def one_chunk(chunk, _):
+        @pl.when(chunk + 1 < chunks)
+        def _():
+            relay(chunk + 1)
+
         for place in range(BLOCKS):
-            halo(chunk, place).wait_recv()
+            if place != FIRST:
+                halo(chunk, place).wait_recv()
+        edge = edge_in[chunk].astype(jnp.float32)
+        for quad in range(CHUNK // QUAD):
+            shift = (channels - quad * EDGE) % channels
+            rows = (pltpu.roll(edge, shift, 0) if shift else edge).astype(jnp.bfloat16)
+            around[chunk, span - channels :, quad * QUAD_LANES : (quad + 1) * QUAD_LANES] = rows
 
         def one_quad(quad, _):
             start = pl.multiple_of(quad * QUAD_LANES, TILE)
@@ -232,6 +277,9 @@
             lanes = slice(half * TILE, (half + 1) * TILE)
             mirrored[half, pl.ds(channel, BLOCKS * channels, stride=channels), :] = back_sum[:, lanes]
 
+    def travels(group, place):
+        return place != LAST or group * few < EDGE
+
     def back(group, place):
         return pltpu.make_async_remote_copy(
             src_ref=back_out.at[group, place],
@@ -244,6 +292,8 @@
 
     for group in range(GROUPS):
         for place in range(BLOCKS):
+            if not travels(group, place):
+                continue
             first = (place * channels + group * few) * channels
             for half in range(LAGS // TILE):
                 rows = mirrored[half, first : first + few * channels].astype(jnp.bfloat16)
@@ -277,7 +327,8 @@
     for group in range(GROUPS + 1):
         if group < GROUPS:
             for place in range(BLOCKS):
-                back(group, place).wait_recv()
+                if travels(group, place):
+                    back(group, place).wait_recv()
             for channel in range(group * few, (group + 1) * few):
                 rows = jnp.dot(chosen[channel], lags[channel], preferred_element_type=jnp.float32)
                 picked[channel] = rows.astype(jnp.bfloat16)
@@ -306,7 +357,8 @@
             halo(chunk, place).wait_send()
     for group in range(GROUPS):
         for place in range(BLOCKS):
-            back(group, place).wait_send()
+            if travels(group, place):
+                back(group, place).wait_send()
         for half in range(2):
             to_core(group, half).wait_send()
         away(group).wait_send()
@@ -340,6 +392,8 @@
             pltpu.VMEM((bins // TILE * channels, 2 * windows * TILE), bf16),
             pltpu.VMEM((chunks, channels, CHUNK_LANES), bf16),
             pltpu.VMEM((chunks, span, CHUNK_LANES), bf16),
+            pltpu.VMEM((chunks, channels, QUAD_LANES), bf16),
+            pltpu.VMEM((chunks, channels, QUAD_LANES), bf16),
             pltpu.VMEM((2, channels, CHUNK, span), bf16),
             pltpu.VMEM((channels, span, LAGS), jnp.float32),
             pltpu.VMEM((channels, span, LAGS), jnp.float32),

time: 91.4 us -> 85.7 us (0.938)
  Pallas kernels: 88.9 us -> 83.3 us
    pallas_call x1, Pallas kernels: 88.9 us -> 83.3 us  [on_device(): pl.pallas_call(kernel, out_shape=jax.ShapeDtypeStruct((LAGS // TILE, shar...]
where the time goes in v4:
time: 85.7 us; the launch traced here: 85.6 us
  Pallas kernels  83.3 us (97%)
  local copies, waits for them, and re-layouts  2.34 us (3%)
    pallas_call x1, Pallas kernels, on_device(): pl.pallas_call(kernel, out_shape=jax.ShapeDtypeStruct((LAGS // TILE, shar...  83.3 us
    reshape x1, local copies, waits for them, and re-layouts, on_device(): return jnp.transpose(stacked, (1, 2, 0, 3)).reshape(share, channels, LAGS)  2.34 us

profile of v4, /device:TPU:1, one launch (start us, length us, event | category | flops | bytes accessed | tf_op | source)
XLA Modules:
  0.0 85.6 jit_solution(16666394311388012940)
XLA Ops:
  0.0 83.3 %stack.1 = f32[2,1024,128]{2,1,0:T(8,128)} custom-call(bf16[2,5,16,1536]{3,2,1,0:T(8,128)(2,1)} %spectra_ref.1, s32[16,256]{1,0:T(8,128)} %partners_ref.1, s32[16,256]{1,0:T(8,128)} %mask_ref.1, s32[16]{0:T(128)} %gap_ref.1, bf16[1024,1024]{1,0:T(8,128)(2,1)} %constant.8.clone.main_ref, bf16[256,256]{1,0:T(8,128)(2,1)} %constant.9.clone.rest_ref, ...), custom_call_target="tpu_custom_call" | custom-call | tf_op jit(solution)/shard_map/stack/pallas_call | solution.py:379
  83.3 2.3 %copy.12 = f32[2,64,2,8,128]{4,3,0,2,1:T(8,128)} copy(f32[2,64,2,8,128]{4,3,2,1,0:T(8,128)} %bitcast.7) | data formatting | bytes 2097152 | tf_op jit(solution)/shard_map/reshape | solution.py:424

commit v5 on v4

--- a/solution.py
+++ b/solution.py
@@ -27,8 +27,10 @@
 QUAD_LANES = 640
 CHUNK = 256
 CHUNK_LANES = CHUNK // QUAD * QUAD_LANES
+RELAYED = 2
+WINDOW = 2
 GROUPS = 8
-ABREAST = 4
+ABREAST = 16
 
 
 def bin_order():
@@ -72,6 +74,11 @@
     other_core = win + 1 - 2 * core
     other_far = lax.rem(win + 2, 4)
 
+    side = 1 - 2 * core
+
+    def offset_of(place):
+        return OFFSETS[place] if place == LAST else side * OFFSETS[place]
+
     def block(offset):
         return lax.rem(me + count + offset, count)
 
@@ -82,8 +89,8 @@
     for load in loads:
         load.start()
     barrier = pltpu.get_barrier_semaphore()
-    for offset in OFFSETS:
-        for chan in (block(offset), block(-offset)):
+    for place in range(BLOCKS):
+        for chan in (block(offset_of(place)), block(-offset_of(place))):
             pl.semaphore_signal(barrier, inc=1, device_id={"chan": chan, "win": win}, device_id_type=MESH)
     for partner in (other_core, other_far):
         pl.semaphore_signal(barrier, inc=1, device_id={"chan": me, "win": partner}, device_id_type=MESH)
@@ -164,19 +171,20 @@
             dst_ref=target,
             send_sem=halo_send.at[chunk, place],
             recv_sem=halo_recv.at[chunk, place],
-            device_id={"chan": block(-RELAY if place == SECOND else -OFFSETS[place]), "win": win},
+            device_id={"chan": block(-side * RELAY if place == SECOND else -offset_of(place)), "win": win},
             device_id_type=MESH,
         )
 
     pl.semaphore_wait(barrier, 2 * BLOCKS + 2)
-    halo(0, FIRST).start()
-    halo(1, FIRST).start()
-    for chunk in range(chunks):
+    def send(chunk):
         for place in range(BLOCKS):
             if place not in (FIRST, SECOND):
                 halo(chunk, place).start()
-        if chunk + 2 < chunks:
-            halo(chunk + 2, FIRST).start()
+
+    for chunk in range(chunks):
+        halo(chunk, FIRST).start()
+    for chunk in range(min(WINDOW, chunks)):
+        send(chunk)
 
     parts = held[...]
     swapped = [parts[:, (i ^ 1) * TILE : ((i ^ 1) + 1) * TILE] for i in range(2 * windows)]
@@ -193,7 +201,8 @@
     loads[windows + 3].wait()
     lane = lax.broadcasted_iota(jnp.int32, (1, 2 * span), 1)
     column = lane
-    for place, offset in enumerate(OFFSETS):
+    for place in range(BLOCKS):
+        offset = offset_of(place)
         column = jnp.where(lane // channels == place + 1, lane + (offset - place - 1) * channels, column)
         column = jnp.where(lane // channels == place + 1 + BLOCKS, lane - (offset + place + 1 + BLOCKS) * channels, column)
     column = jnp.where(lane // channels == 2 * BLOCKS + 1, 2**20, column).astype(jnp.float32)
@@ -217,12 +226,17 @@
         halo(chunk, FIRST).wait_recv()
         halo(chunk, SECOND).start()
 
-    relay(0)
+    for chunk in range(min(RELAYED, chunks)):
+        relay(chunk)
 
     def one_chunk(chunk, _):
-        @pl.when(chunk + 1 < chunks)
+        @pl.when(chunk + RELAYED < chunks)
         def _():
-            relay(chunk + 1)
+            relay(chunk + RELAYED)
+
+        @pl.when(chunk + WINDOW < chunks)
+        def _():
+            send(chunk + WINDOW)
 
         for place in range(BLOCKS):
             if place != FIRST:
@@ -243,14 +257,14 @@
 
             for group in range(QUAD // SUB):
                 others = lane_tiles(around, span, group)
-                for part, ref in ((0, around), (1, turned)):
-                    own = lane_tiles(ref, channels, group)
-                    spread = (own[:, None, :] * masks[group][None, :, :]).reshape(channels * SUB, 2 * TILE)
-                    product = lax.dot_general(
-                        spread, others, (((1,), (1,)), ((), ())), preferred_element_type=jnp.float32
-                    )
-                    first_bin = pl.multiple_of(quad * QUAD + group * SUB, SUB)
-                    cross[part, :, pl.ds(first_bin, SUB), :] = product.astype(jnp.bfloat16).reshape(channels, SUB, span)
+                own = jnp.concatenate([lane_tiles(ref, channels, group) for ref in (around, turned)], axis=0)
+                spread = (own[:, None, :] * masks[group][None, :, :]).reshape(2 * channels * SUB, 2 * TILE)
+                product = lax.dot_general(
+                    spread, others, (((1,), (1,)), ((), ())), preferred_element_type=jnp.float32
+                )
+                first_bin = pl.multiple_of(quad * QUAD + group * SUB, SUB)
+                product = product.astype(jnp.bfloat16).reshape(2, channels, SUB, span)
+                cross[:, :, pl.ds(first_bin, SUB), :] = product
             return 0
 
         lax.fori_loop(0, CHUNK // QUAD, one_quad, 0)
@@ -286,7 +300,7 @@
             dst_ref=lags.at[pl.ds(group * few, few), pl.ds(span + place * channels, channels), :],
             send_sem=back_send.at[group, place],
             recv_sem=back_recv.at[group, place],
-            device_id={"chan": block(OFFSETS[place]), "win": win},
+            device_id={"chan": block(offset_of(place)), "win": win},
             device_id_type=MESH,
         )
 

time: 85.7 us -> 81.2 us (0.947)
  Pallas kernels: 83.3 us -> 78.7 us
    pallas_call x1, Pallas kernels: 83.3 us -> 78.7 us  [on_device(): pl.pallas_call(kernel, out_shape=jax.ShapeDtypeStruct((LAGS // TILE, shar...]
where the time goes in v5:
time: 81.2 us; the launch traced here: 81 us
  Pallas kernels  78.7 us (97%)
  local copies, waits for them, and re-layouts  2.34 us (3%)
    pallas_call x1, Pallas kernels, on_device(): pl.pallas_call(kernel, out_shape=jax.ShapeDtypeStruct((LAGS // TILE, shar...  78.7 us
    reshape x1, local copies, waits for them, and re-layouts, on_device(): return jnp.transpose(stacked, (1, 2, 0, 3)).reshape(share, channels, LAGS)  2.34 us

profile of v5, /device:TPU:1, one launch (start us, length us, event | category | flops | bytes accessed | tf_op | source)
XLA Modules:
  0.0 81.0 jit_solution(10390001604630296905)
XLA Ops:
  0.0 78.7 %stack.1 = f32[2,1024,128]{2,1,0:T(8,128)} custom-call(bf16[2,5,16,1536]{3,2,1,0:T(8,128)(2,1)} %spectra_ref.1, s32[16,256]{1,0:T(8,128)} %partners_ref.1, s32[16,256]{1,0:T(8,128)} %mask_ref.1, s32[16]{0:T(128)} %gap_ref.1, bf16[1024,1024]{1,0:T(8,128)(2,1)} %constant.8.clone.main_ref, bf16[256,256]{1,0:T(8,128)(2,1)} %constant.9.clone.rest_ref, ...), custom_call_target="tpu_custom_call" | custom-call | tf_op jit(solution)/shard_map/stack/pallas_call | solution.py:393
  78.7 2.3 %copy.12 = f32[2,64,2,8,128]{4,3,0,2,1:T(8,128)} copy(f32[2,64,2,8,128]{4,3,2,1,0:T(8,128)} %bitcast.7) | data formatting | bytes 2097152 | tf_op jit(solution)/shard_map/reshape | solution.py:438

commit v6 on v5

--- a/solution.py
+++ b/solution.py
@@ -1,3 +1,4 @@
+import functools
 import math
 
 import jax
@@ -19,6 +20,8 @@
 BLOCKS = len(OFFSETS)
 FIRST, SECOND = 1, 5
 RELAY = OFFSETS[SECOND] - OFFSETS[FIRST]
+NEXT, THIRD, ROW = 0, 2, 3
+WIDE = 4
 LAST = BLOCKS - 1
 EDGE = 4
 TILE = 128
@@ -27,6 +30,7 @@
 QUAD_LANES = 640
 CHUNK = 256
 CHUNK_LANES = CHUNK // QUAD * QUAD_LANES
+EARLY = 4
 RELAYED = 2
 WINDOW = 2
 GROUPS = 8
@@ -55,7 +59,7 @@
 
 def kernel(
     spectra_ref, partners_ref, mask_ref, gap_ref, main_ref, rest_ref, cos_ref, sin_ref, out_ref,
-    spectra, partners, mask, main, rest, cos_table, sin_table,
+    spectra, gap, partners, mask, main, rest, cos_table, sin_table,
     held, turned, around, edge_out, edge_in, cross, even, odd, chosen, mirrored, lags, back_out, picked, from_core, to_far, from_far,
     load_sem, halo_send, halo_recv, back_send, back_recv, core_send, core_recv, far_send, far_recv,
 ):
@@ -82,11 +86,12 @@
     def block(offset):
         return lax.rem(me + count + offset, count)
 
-    loads = [(spectra_ref.at[:, window], spectra.at[:, window]) for window in range(windows)]
+    loads = [(gap_ref, gap), (spectra_ref.at[:, 0], spectra.at[:, 0])]
+    loads += [(spectra_ref.at[:, window], spectra.at[:, window]) for window in range(1, windows)]
     loads += [(main_ref, main), (rest_ref, rest), (partners_ref, partners), (mask_ref, mask)]
     loads += [(cos_ref, cos_table), (sin_ref, sin_table)]
     loads = [pltpu.make_async_copy(source, target, load_sem.at[i]) for i, (source, target) in enumerate(loads)]
-    for load in loads:
+    for load in loads[: windows + 3]:
         load.start()
     barrier = pltpu.get_barrier_semaphore()
     for place in range(BLOCKS):
@@ -98,13 +103,14 @@
     position = lax.broadcasted_iota(jnp.int32, (1, bins), 1)
     bin_count = jnp.minimum(position + SMOOTH, bins - 1) - jnp.maximum(position - SMOOTH, 0) + 1
     inverse = 1.0 / bin_count.astype(jnp.float32)
-    row = lax.broadcasted_iota(jnp.int32, (channels, 1), 0)
-    live = jnp.zeros((channels, 1), jnp.float32)
-    for channel in range(channels):
-        live = jnp.where(row == channel, jnp.where(gap_ref[channel] == 0, 1.0, 0.0), live)
+    loads[0].wait()
+    row = lax.broadcasted_iota(jnp.int32, (channels, channels), 0)
+    lane = lax.broadcasted_iota(jnp.int32, (channels, channels), 1)
+    live = jnp.where((row == lane) & (gap[...] == 0), 1.0, 0.0)
+    live = jnp.sum(live, axis=1, keepdims=True)
     pad = jnp.zeros((channels, TILE), jnp.float32)
     for window in range(windows):
-        loads[window].wait()
+        loads[window + 1].wait()
         real_part = spectra[0, window].astype(jnp.float32)
         imag_part = spectra[1, window].astype(jnp.float32)
         magnitude = jnp.sqrt(real_part * real_part + imag_part * imag_part)
@@ -146,8 +152,8 @@
     def store_turned(chunk, lanes, value):
         turned[chunk, :, lanes] = value
 
-    loads[windows].wait()
     loads[windows + 1].wait()
+    loads[windows + 2].wait()
     wide_first, wide_last = ordered(held[...], store_around)
     for chunk in range(chunks):
         pieces = []
@@ -159,32 +165,54 @@
             pieces.append(jnp.concatenate([first, last], axis=1))
         edge_out[chunk] = jnp.concatenate(pieces, axis=0).astype(jnp.bfloat16)
 
-    def halo(chunk, place):
+    def column_of(chan):
+        x = lax.rem(chan, WIDE)
+        return x + core * (WIDE - 1 - 2 * x)
+
+    def halo(chunk, place, relayed=False):
+        to, sent = block(-offset_of(place)), place
+        if place == SECOND:
+            to = block(-side * RELAY)
+        if relayed:
+            to, sent = block(side * (WIDE - OFFSETS[place])), BLOCKS + place // 2
         if place == LAST:
             source, target = edge_out.at[chunk], edge_in.at[chunk]
         else:
-            first = (FIRST + 1) * channels if place == SECOND else 0
+            first = (ROW + 1) * channels if relayed else (FIRST + 1) * channels if place == SECOND else 0
             source = around.at[chunk, pl.ds(first, channels), :]
             target = around.at[chunk, pl.ds((place + 1) * channels, channels), :]
         return pltpu.make_async_remote_copy(
             src_ref=source,
             dst_ref=target,
-            send_sem=halo_send.at[chunk, place],
+            send_sem=halo_send.at[chunk, sent],
             recv_sem=halo_recv.at[chunk, place],
-            device_id={"chan": block(-side * RELAY if place == SECOND else -offset_of(place)), "win": win},
+            device_id={"chan": to, "win": win},
             device_id_type=MESH,
         )
 
+    def at_places(act, relayed):
+        for place in (NEXT, THIRD):
+            to = block(side * (WIDE - OFFSETS[place]) if relayed else -offset_of(place))
+            from_row = column_of(to) >= (WIDE - 1 if place == NEXT else 1)
+            pl.when(from_row if relayed else jnp.logical_not(from_row))(functools.partial(act, place))
+
     pl.semaphore_wait(barrier, 2 * BLOCKS + 2)
     def send(chunk):
+        at_places(lambda place: halo(chunk, place).start(), False)
         for place in range(BLOCKS):
-            if place not in (FIRST, SECOND):
+            if place not in (FIRST, SECOND, NEXT, THIRD, ROW):
                 halo(chunk, place).start()
 
-    for chunk in range(chunks):
+    def send_early(chunk):
+        halo(chunk, ROW).start()
         halo(chunk, FIRST).start()
+
+    for chunk in range(min(EARLY, chunks)):
+        send_early(chunk)
     for chunk in range(min(WINDOW, chunks)):
         send(chunk)
+    for load in loads[windows + 3 :]:
+        load.start()
 
     parts = held[...]
     swapped = [parts[:, (i ^ 1) * TILE : ((i ^ 1) + 1) * TILE] for i in range(2 * windows)]
@@ -197,8 +225,8 @@
         (channels - EDGE, channels, LAGS), jnp.bfloat16
     )
 
-    loads[windows + 2].wait()
     loads[windows + 3].wait()
+    loads[windows + 4].wait()
     lane = lax.broadcasted_iota(jnp.int32, (1, 2 * span), 1)
     column = lane
     for place in range(BLOCKS):
@@ -219,10 +247,12 @@
         first = (lane % SUB == row).astype(jnp.float32)
         last = (lane % QUAD == group * SUB + row).astype(jnp.float32)
         masks.append(jnp.concatenate([first, last], axis=1).astype(jnp.bfloat16))
-    loads[windows + 4].wait()
     loads[windows + 5].wait()
+    loads[windows + 6].wait()
 
     def relay(chunk):
+        halo(chunk, ROW).wait_recv()
+        at_places(lambda place: halo(chunk, place, True).start(), True)
         halo(chunk, FIRST).wait_recv()
         halo(chunk, SECOND).start()
 
@@ -234,12 +264,16 @@
         def _():
             relay(chunk + RELAYED)
 
+        @pl.when(chunk + EARLY < chunks)
+        def _():
+            send_early(chunk + EARLY)
+
         @pl.when(chunk + WINDOW < chunks)
         def _():
             send(chunk + WINDOW)
 
         for place in range(BLOCKS):
-            if place != FIRST:
+            if place not in (FIRST, ROW):
                 halo(chunk, place).wait_recv()
         edge = edge_in[chunk].astype(jnp.float32)
         for quad in range(CHUNK // QUAD):
@@ -367,8 +401,11 @@
                 out_ref[half, pl.ds(channel, share, stride=channels), :] = ((mine + theirs) * scale)[:, lanes]
 
     for chunk in range(chunks):
+        for relayed in (False, True):
+            at_places(lambda place, relayed=relayed: halo(chunk, place, relayed).wait_send(), relayed)
         for place in range(BLOCKS):
-            halo(chunk, place).wait_send()
+            if place not in (NEXT, THIRD):
+                halo(chunk, place).wait_send()
     for group in range(GROUPS):
         for place in range(BLOCKS):
             if travels(group, place):
@@ -388,15 +425,15 @@
     main, rest = bin_order()
     cos_table, sin_table = lag_tables(bins)
     anywhere = pl.BlockSpec(memory_space=pl.ANY)
-    scalars = pl.BlockSpec(memory_space=pltpu.SMEM)
     semaphores = pltpu.SemaphoreType.DMA
     stacked = pl.pallas_call(
         kernel,
         out_shape=jax.ShapeDtypeStruct((LAGS // TILE, share * channels, TILE), jnp.float32),
-        in_specs=[anywhere] * 3 + [scalars] + [anywhere] * 4,
+        in_specs=[anywhere] * 8,
         out_specs=pl.BlockSpec(memory_space=pltpu.VMEM),
         scratch_shapes=[
             pltpu.VMEM(spectra.shape, bf16),
+            pltpu.VMEM((1, channels), jnp.int32),
             pltpu.VMEM(partners.shape, jnp.int32),
             pltpu.VMEM(pair_mask.shape, jnp.int32),
             pltpu.VMEM(main.shape, bf16),
@@ -419,8 +456,8 @@
             pltpu.VMEM((2, channels, share, LAGS), bf16),
             pltpu.VMEM((channels, share, LAGS), bf16),
             pltpu.VMEM((channels, share, LAGS), bf16),
-            semaphores((windows + 6,)),
-            semaphores((chunks, BLOCKS)),
+            semaphores((windows + 7,)),
+            semaphores((chunks, BLOCKS + 2)),
             semaphores((chunks, BLOCKS)),
             semaphores((GROUPS, BLOCKS)),
             semaphores((GROUPS, BLOCKS)),
@@ -433,7 +470,7 @@
             collective_id=0, has_side_effects=True, vmem_limit_bytes=56 * 2**20
         ),
         name="stack",
-    )(spectra, partners, pair_mask, gap_flags, main, rest, cos_table, sin_table)
+    )(spectra, partners, pair_mask, gap_flags[None, :], main, rest, cos_table, sin_table)
     stacked = stacked.reshape(LAGS // TILE, share, channels, TILE)
     return jnp.transpose(stacked, (1, 2, 0, 3)).reshape(share, channels, LAGS)
 

time: 81.2 us -> 74.6 us (0.919)
  Pallas kernels: 78.7 us -> 72.1 us
    pallas_call x1, Pallas kernels: 78.7 us -> 72.1 us  [on_device(): pl.pallas_call(kernel, out_shape=jax.ShapeDtypeStruct((LAGS // TILE, shar...]
where the time goes in v6:
time: 74.6 us; the launch traced here: 74.4 us
  Pallas kernels  72.1 us (97%)
  local copies, waits for them, and re-layouts  2.34 us (3%)
    pallas_call x1, Pallas kernels, on_device(): pl.pallas_call(kernel, out_shape=jax.ShapeDtypeStruct((LAGS // TILE, shar...  72.1 us
    reshape x1, local copies, waits for them, and re-layouts, on_device(): return jnp.transpose(stacked, (1, 2, 0, 3)).reshape(share, channels, LAGS)  2.34 us

profile of v6, /device:TPU:1, one launch (start us, length us, event | category | flops | bytes accessed | tf_op | source)
XLA Modules:
  0.0 74.4 jit_solution(11875890123249736759)
XLA Ops:
  0.0 72.1 %stack.1 = f32[2,1024,128]{2,1,0:T(8,128)} custom-call(bf16[2,5,16,1536]{3,2,1,0:T(8,128)(2,1)} %spectra_ref.1, s32[16,256]{1,0:T(8,128)} %partners_ref.1, s32[16,256]{1,0:T(8,128)} %mask_ref.1, s32[1,16]{1,0:T(1,128)} %bitcast.9, bf16[1024,1024]{1,0:T(8,128)(2,1)} %constant.8.clone.main_ref, bf16[256,256]{1,0:T(8,128)(2,1)} %constant.9.clone.rest_ref, ...), custom_call_target="tpu_custom_call" | custom-call | tf_op jit(solution)/shard_map/stack/pallas_call | solution.py:429
  72.1 2.3 %copy.12 = f32[2,64,2,8,128]{4,3,0,2,1:T(8,128)} copy(f32[2,64,2,8,128]{4,3,2,1,0:T(8,128)} %bitcast.8) | data formatting | bytes 2097152 | tf_op jit(solution)/shard_map/reshape | solution.py:475

commit v7 on v6

--- a/solution.py
+++ b/solution.py
@@ -260,17 +260,17 @@
         relay(chunk)
 
     def one_chunk(chunk, _):
+        @pl.when(chunk + WINDOW < chunks)
+        def _():
+            send(chunk + WINDOW)
+
+        @pl.when(chunk + EARLY < chunks)
+        def _():
+            send_early(chunk + EARLY)
+
         @pl.when(chunk + RELAYED < chunks)
         def _():
             relay(chunk + RELAYED)
-
-        @pl.when(chunk + EARLY < chunks)
-        def _():
-            send_early(chunk + EARLY)
-
-        @pl.when(chunk + WINDOW < chunks)
-        def _():
-            send(chunk + WINDOW)
 
         for place in range(BLOCKS):
             if place not in (FIRST, ROW):
@@ -338,8 +338,9 @@
             device_id_type=MESH,
         )
 
+    longest_first = (SECOND, FIRST, LAST, 4, THIRD, NEXT, ROW)
     for group in range(GROUPS):
-        for place in range(BLOCKS):
+        for place in longest_first:
             if not travels(group, place):
                 continue
             first = (place * channels + group * few) * channels

time: 74.6 us -> 74.2 us (level)
  no operation moved by 1% of the time
where the time goes in v7:
time: 74.2 us; the launch traced here: 74.1 us
  Pallas kernels  71.7 us (97%)
  local copies, waits for them, and re-layouts  2.34 us (3%)
    pallas_call x1, Pallas kernels, on_device(): pl.pallas_call(kernel, out_shape=jax.ShapeDtypeStruct((LAGS // TILE, shar...  71.7 us
    reshape x1, local copies, waits for them, and re-layouts, on_device(): return jnp.transpose(stacked, (1, 2, 0, 3)).reshape(share, channels, LAGS)  2.34 us

profile of v7, /device:TPU:1, one launch (start us, length us, event | category | flops | bytes accessed | tf_op | source)
XLA Modules:
  0.0 74.1 jit_solution(3356627994420144815)
XLA Ops:
  0.0 71.7 %stack.1 = f32[2,1024,128]{2,1,0:T(8,128)} custom-call(bf16[2,5,16,1536]{3,2,1,0:T(8,128)(2,1)} %spectra_ref.1, s32[16,256]{1,0:T(8,128)} %partners_ref.1, s32[16,256]{1,0:T(8,128)} %mask_ref.1, s32[1,16]{1,0:T(1,128)} %bitcast.9, bf16[1024,1024]{1,0:T(8,128)(2,1)} %constant.8.clone.main_ref, bf16[256,256]{1,0:T(8,128)(2,1)} %constant.9.clone.rest_ref, ...), custom_call_target="tpu_custom_call" | custom-call | tf_op jit(solution)/shard_map/stack/pallas_call | solution.py:430
  71.7 2.3 %copy.12 = f32[2,64,2,8,128]{4,3,0,2,1:T(8,128)} copy(f32[2,64,2,8,128]{4,3,2,1,0:T(8,128)} %bitcast.8) | data formatting | bytes 2097152 | tf_op jit(solution)/shard_map/reshape | solution.py:476
